TPU v7x, 32 devices: a whole 2x2x4 slice. The times are simulated.
32 devices in a mesh: rep: 8 (over y, x, core), zero: 4 (over z).
Axes of the slice: x: 2, y: 2, z: 4, core: 2. Of those that a mesh axis runs over, the one named last changes fastest.
Arguments:
- tokens: bfloat16 [8192, 1024], P(('rep', 'zero')), may hold values from -6 to 6
- cotangent: bfloat16 [8192, 1024], P(('rep', 'zero')), may hold values from -6 to 6
- seq_len: int32 [128], replicated, may hold values from 0 to 256, as said below
- seq_dev: int32 [128], replicated, may hold values from 0 to 31, as said below
- seq_off: int32 [128], replicated, may hold values from 0 to 256, as said below
- params: float32 [18355200], P(('rep', 'zero'))
- first_moment: float32 [18355200], P(('rep', 'zero'))
- second_moment: float32 [18355200], P(('rep', 'zero'))
Outputs:
- mixed: bfloat16 [8192, 1024], P(('rep', 'zero'))
- token_grad: bfloat16 [8192, 1024], P(('rep', 'zero'))
- param_grad: float32 [18355200], P(('rep', 'zero'))
- small_grad: float32 [5120], P(('rep', 'zero'))
- second_new: float32 [18355200], P(('rep', 'zero'))
- params_new: float32 [18355200], P(('rep', 'zero'))
Inputs may be any that keep to these rules, and one draw needn't show every extreme that they name: `seq_len`: length of a record, 0 for an unused one. The records of one device lie one after another from slot 0 in the order of their seq_off and fill at most 256 slots; in every draw some device is full with a single record of length 256. `seq_dev`: device index in rep-major order; every device holds exactly 4 records. `seq_off`: A record's first slot on its device; records of a device do not intersect.
All inputs are finite; a program needn't handle non-finite values.
Results may differ from a plain program's by a relative error of at most 0.012.
Values may be sent and summed in bfloat16 or wider, within the bound.
No kernel may reach another device: no remote copies, remote signals or barrier semaphores. Data moves between devices by JAX's collectives and lax.ppermute only.
A program may use at most 320 MiB of HBM per device.

v0:
```python
import jax
import jax.numpy as jnp
from jax import lax
from jax.sharding import PartitionSpec as P

D = 1024
FF = 4608
STEP = 10


norm_epsilon = 1e-05
first_decay = 0.9
second_decay = 0.999
moment_epsilon = 1e-08
weight_decay = 0.1
learn_rate = 0.06


def segment_sizes():
    return (3 * D * D, D * D, 2 * D * FF, FF * D, 5 * D)


def unpack_whole(vector, shards):
    table = vector.reshape(shards, -1)
    pieces = []
    offset = 0
    for extent in segment_sizes():
        columns = extent // shards
        pieces.append(table[:, offset : offset + columns].reshape(-1))
        offset = offset + columns
    return pieces


def pack_whole(pieces, shards):
    return jnp.concatenate([segment.reshape(shards, -1) for segment in pieces], axis=1).reshape(-1)


def layout(starts, lengths, slot_count):
    nonempty = lengths > 0
    opening = jnp.where(nonempty, starts, slot_count)
    closing = jnp.where(nonempty, starts + lengths, slot_count)
    markers = jnp.full((slot_count,), -1, jnp.int32).at[opening].max(starts, mode="drop")
    latest = lax.cummax(markers, axis=0)
    position = jnp.arange(slot_count, dtype=jnp.int32) - latest
    boundary = (
        jnp.zeros((slot_count,), jnp.int32)
        .at[opening]
        .add(1, mode="drop")
        .at[closing]
        .add(-1, mode="drop")
    )
    occupied = jnp.cumsum(boundary) > 0
    return (position, occupied)


def rms_scale(values):
    return lax.rsqrt(jnp.mean(values * values, axis=-1, keepdims=True) + norm_epsilon)


def shift_down(values, steps):
    return jnp.pad(values, ((steps, 0), (0, 0)))[: values.shape[0]]


def shift_up(values, steps):
    return jnp.pad(values, ((0, steps), (0, 0)))[steps:]


def matmul(left, right):
    return jnp.dot(left, right, preferred_element_type=jnp.float32)


def over_rows(left, right):
    return lax.dot_general(
        left, right, (((0,), (0,)), ((), ())), preferred_element_type=jnp.float32
    )


def against(left, right):
    return lax.dot_general(
        left, right, (((1,), (1,)), ((), ())), preferred_element_type=jnp.float32
    )


def local(tokens, cotangent, seq_len, seq_dev, seq_off, params, first_moment, second_moment):
    shards = lax.axis_size(("rep", "zero"))
    device = lax.axis_index(("rep", "zero"))
    slot_count = tokens.shape[0]
    share = params.astype(jnp.bfloat16)
    gathered = lax.all_gather(share, ("rep", "zero"), axis=0, tiled=True)
    pieces = unpack_whole(gathered, shards)
    weight_in = pieces[0].reshape(D, 3 * D)
    weight_out = pieces[1].reshape(D, D)
    weight_gateup = pieces[2].reshape(D, 2 * FF)
    weight_down = pieces[3].reshape(FF, D)
    small_params = pieces[4].reshape(5, D).astype(jnp.float32)
    gain_one = small_params[0]
    gain_two = small_params[1]
    mine = seq_dev == device
    position, occupied = layout(
        jnp.where(mine, seq_off, slot_count), jnp.where(mine, seq_len, 0), slot_count
    )
    keeper = occupied.astype(jnp.float32)[:, None]
    reach_one = (occupied & (position >= 1)).astype(jnp.float32)[:, None]
    reach_two = (occupied & (position >= 2)).astype(jnp.float32)[:, None]
    inputs = tokens.astype(jnp.float32)
    scale_one = rms_scale(inputs)
    unit_one = inputs * scale_one
    normed = (unit_one * gain_one).astype(jnp.bfloat16)
    mixin = matmul(normed, weight_in)
    b_part = mixin[:, :D]
    c_part = mixin[:, D : 2 * D]
    v_part = mixin[:, 2 * D :]
    product = b_part * v_part
    lag_one = shift_down(product, 1) * reach_one
    lag_two = shift_down(product, 2) * reach_two
    convolved = small_params[2] * product + small_params[3] * lag_one + small_params[4] * lag_two
    gated = (c_part * convolved).astype(jnp.bfloat16)
    branch = matmul(gated, weight_out)
    middle = inputs + keeper * branch
    scale_two = rms_scale(middle)
    unit_two = middle * scale_two
    normed_two = (unit_two * gain_two).astype(jnp.bfloat16)
    gate_up = matmul(normed_two, weight_gateup)
    gate_part = gate_up[:, :FF]
    up_part = gate_up[:, FF:]
    sigma = jax.nn.sigmoid(gate_part)
    swish = gate_part * sigma
    hidden = (swish * up_part).astype(jnp.bfloat16)
    feed_out = matmul(hidden, weight_down)
    mixed = (middle + keeper * feed_out).astype(jnp.bfloat16)
    upstream = cotangent.astype(jnp.float32)
    feed_back = (keeper * upstream).astype(jnp.bfloat16)
    grad_down = over_rows(hidden, feed_back)
    hidden_back = against(feed_back, weight_down)
    gate_back = hidden_back * up_part * (sigma + gate_part * sigma * (1.0 - sigma))
    up_back = hidden_back * swish
    gateup_back = jnp.concatenate([gate_back, up_back], axis=1).astype(jnp.bfloat16)
    grad_gateup = over_rows(normed_two, gateup_back)
    normed_two_back = against(gateup_back, weight_gateup)
    grad_gain_two = jnp.sum(normed_two_back * unit_two, axis=0)
    unit_two_back = normed_two_back * gain_two
    middle_back = upstream + scale_two * (
        unit_two_back - unit_two * jnp.mean(unit_two_back * unit_two, axis=-1, keepdims=True)
    )
    branch_back = (keeper * middle_back).astype(jnp.bfloat16)
    grad_out = over_rows(gated, branch_back)
    gated_back = against(branch_back, weight_out)
    conv_back = gated_back * c_part
    c_back = gated_back * convolved
    grad_tap_zero = jnp.sum(conv_back * product, axis=0)
    grad_tap_one = jnp.sum(conv_back * lag_one, axis=0)
    grad_tap_two = jnp.sum(conv_back * lag_two, axis=0)
    product_back = (
        small_params[2] * conv_back
        + shift_up(small_params[3] * conv_back * reach_one, 1)
        + shift_up(small_params[4] * conv_back * reach_two, 2)
    )
    mixin_back = jnp.concatenate(
        [product_back * v_part, c_back, product_back * b_part], axis=1
    ).astype(jnp.bfloat16)
    grad_in = over_rows(normed, mixin_back)
    normed_back = against(mixin_back, weight_in)
    grad_gain_one = jnp.sum(normed_back * unit_one, axis=0)
    unit_one_back = normed_back * gain_one
    inputs_back = middle_back + scale_one * (
        unit_one_back - unit_one * jnp.mean(unit_one_back * unit_one, axis=-1, keepdims=True)
    )
    token_grad = inputs_back.astype(jnp.bfloat16)
    small_terms = jnp.stack(
        [grad_gain_one, grad_gain_two, grad_tap_zero, grad_tap_one, grad_tap_two], axis=0
    )
    local_terms = pack_whole([grad_in, grad_out, grad_gateup, grad_down, small_terms], shards)
    param_grad = lax.psum_scatter(local_terms, ("rep", "zero"), scatter_dimension=0, tiled=True)
    shard_len = params.shape[0]
    matrix_len = shard_len - 5 * D // shards
    small_grad = param_grad[matrix_len:]
    matrix_mask = (jnp.arange(shard_len) < matrix_len).astype(jnp.float32)
    moment = first_decay * first_moment + (1.0 - first_decay) * param_grad
    second_new = second_decay * second_moment + (1.0 - second_decay) * param_grad * param_grad
    moment_hat = moment / (1.0 - first_decay**STEP)
    second_hat = second_new / (1.0 - second_decay**STEP)
    params_new = params - learn_rate * (
        moment_hat / (jnp.sqrt(second_hat) + moment_epsilon) + weight_decay * matrix_mask * params
    )
    return (mixed, token_grad, param_grad, small_grad, second_new, params_new)


def solution(mesh):
    placed = (
        P(("rep", "zero"), None),
        P(("rep", "zero"), None),
        P(),
        P(),
        P(),
        P(("rep", "zero")),
        P(("rep", "zero")),
        P(("rep", "zero")),
    )
    return jax.shard_map(
        local,
        mesh=mesh,
        in_specs=placed,
        out_specs=(
            P(("rep", "zero"), None),
            P(("rep", "zero"), None),
            P(("rep", "zero")),
            P(("rep", "zero")),
            P(("rep", "zero")),
            P(("rep", "zero")),
        ),
        check_vma=False,
    )
```

profile of v0, /device:TPU:0, one launch (start us, length us, event | category | flops | bytes accessed | tf_op | source)
XLA Modules:
  0.0 2107.6 jit_solution(10919871970909101420)
XLA Ops:
  9.0 11.9 broadcast.105
  20.9 18.3 dynamic-update-slice
  46.1 537.8 %all-reduce.9.cloned.1.call-done = bf16[18355200]{0:T(1024)(128)(2,1)} async-done(((bf16[18355200]{0:T(1024)(128)(2,1)}), bf16[18355200]{0:T(1024)(128)(2,1)}) %all-reduce.9.cloned.1.call-update) | async-done | bytes 36710416
  584.0 72.1 %reshape.141 = bf16[32,573600]{1,0:T(8,128)(2,1)} reshape(bf16[18355200]{0:T(1024)(128)(2,1)} %all-reduce.9.cloned.1.call-done) | data formatting | bytes 73420800 | tf_op jit(solution)/shard_map/reshape | solution.py:24
  662.6 17.6 slice.112
  690.7 7.3 reshape_reshape.13
  708.7 26.6 %reshape_reshape.15 = bf16[1024,9216]{1,0:T(8,128)(2,1)} reshape(bf16[32,294912]{1,0:T(8,128)(2,1)} %slice.112) | data formatting | bytes 37748736 | tf_op jit(solution)/shard_map/reshape;reshape | solution.py:93
  740.6 9.7 reshape_reshape.16
  750.3 9.4 fusion.43
  759.7 12.8 multiply_convert_fusion.1
  772.6 11.7 multiply_reduce_fusion.3
  795.3 6.5 fusion.22
  804.7 16.5 fusion
  821.2 9.8 reshape.144
  831.0 9.9 constant_dynamic-update-slice_fusion.4
  845.9 36.1 %reshape.146 = f32[32,294912]{1,0:T(8,128)} reshape(f32[1024,9216]{1,0:T(8,128)} %fusion) | data formatting | bytes 75497472 | tf_op jit(solution)/shard_map/reshape | solution.py:35
  882.0 8.0 fusion.24
  890.0 21.3 %reshape.147 = f32[32,147456]{1,0:T(8,128)} reshape(f32[4608,1024]{1,0:T(8,128)} %fusion.24) | data formatting | bytes 37748736 | tf_op jit(solution)/shard_map/reshape | solution.py:35
  916.1 30.1 %constant_dynamic-update-slice_fusion.2 = f32[32,573600]{1,0:T(8,128)} fusion(f32[32,573600]{1,0:T(8,128)} %constant_dynamic-update-slice_fusion.3, f32[32,294912]{1,0:T(8,128)} %reshape.146), kind=kLoop, calls=%fused_computation.71 | loop fusion | bytes 75497472
  946.2 6.7 constant_dynamic-update-slice_fusion.1
  953.6 85.6 %reshape.149 = f32[18355200]{0:T(1024)} reshape(f32[32,573600]{1,0:T(8,128)} %constant_dynamic-update-slice_fusion) | data formatting | bytes 146841600 | tf_op jit(solution)/shard_map/reshape | solution.py:35
  1042.9 8.8 fusion.8
  1051.7 1039.0 %all-reduce.11.cloned.1.call-done = f32[18355200]{0:T(1024)} async-done(((f32[18355200]{0:T(1024)}), f32[18355200]{0:T(1024)}) %all-reduce.11.cloned.1.call-update) | async-done | bytes 73420816
  2092.0 8.6 multiply_subtract_fusion
  (125 shorter events, 70.8 us)
Async XLA Ops:
  7.2 576.8 %all-reduce.9.cloned.1.call-start = ((), (), s32[]{:S(2)}) async-start(), calls=%async_computation | async-start | bytes 73420800
  39.2 6.6 copy-start.10
  39.2 2051.4 %all-reduce.11.cloned.1.call-start = ((), (), s32[]{:S(2)}) async-start(), calls=%async_computation.1 | async-start | bytes 146841600
  46.0 749.3 %copy-start.22 = (f32[256]{0:T(256)}, f32[256]{0:T(256)S(1)}, u32[]{:S(2)}) copy-start(f32[256]{0:T(256)S(1)} %add_rsqrt_fusion.1) | copy-start | bytes 3076
  662.6 23.9 %copy-start = (bf16[32,573600]{1,0:T(8,128)(2,1)S(1)}, bf16[32,573600]{1,0:T(8,128)(2,1)}, u32[]{:S(2)}) copy-start(bf16[32,573600]{1,0:T(8,128)(2,1)} %reshape.141) | copy-start | bytes 110131200
  698.1 97.3 %copy-start.20 = (f32[1,1024]{1,0:T(1,128)}, f32[1,1024]{1,0:T(1,128)S(1)}, u32[]{:S(2)}) copy-start(f32[1,1024]{1,0:T(1,128)S(1)} %get-tuple-element.35) | copy-start | bytes 12292
  708.7 26.7 %copy-start.4 = (f32[256,3072]{1,0:T(8,128)S(1)}, f32[256,3072]{1,0:T(8,128)}, u32[]{:S(2)}) copy-start(f32[256,3072]{1,0:T(8,128)} %copy-done.3) | copy-start | bytes 9437188
  735.3 3.5 copy-start.8
  735.3 3.5 copy-start.11
  750.3 9.4 copy-start.16
  759.7 12.8 copy-start.5
  786.0 15.8 copy-start.1
  789.2 2.6 slice-start.7
  789.2 2.7 copy-start.12
  795.3 6.5 copy-start.19
  801.8 2.8 copy-start.14
  845.9 36.1 %copy-start.15 = (bf16[256,4608]{1,0:T(8,128)(2,1)S(1)}, bf16[256,4608]{1,0:T(8,128)(2,1)}, u32[]{:S(2)}) copy-start(bf16[256,4608]{1,0:T(8,128)(2,1)} %get-tuple-element.27) | copy-start | bytes 7077892
  845.9 36.1 %copy-start.17 = (bf16[256,1024]{1,0:T(8,128)(2,1)S(1)}, bf16[256,1024]{1,0:T(8,128)(2,1)}, u32[]{:S(2)}) copy-start(bf16[256,1024]{1,0:T(8,128)(2,1)} %param.9) | copy-start | bytes 1572868
  911.4 34.8 %slice-start.1 = ((s8[18874368]{0:T(1024)(128)(4,1)}), s8[4194304]{0:T(1024)(128)(4,1)S(1)}, s32[]{:S(2)}) async-start(s8[18874368]{0:T(1024)(128)(4,1)} %bitcast.39), calls=%async_computation.3 | async-start | bytes 8388608
  916.1 30.2 %slice-start.2 = ((s8[18874368]{0:T(1024)(128)(4,1)}), s8[4194304]{0:T(1024)(128)(4,1)S(1)}, s32[]{:S(2)}) async-start(s8[18874368]{0:T(1024)(128)(4,1)} %bitcast.39), calls=%async_computation.4 | async-start | bytes 8388608
  916.1 30.2 %slice-start.3 = ((s8[18874368]{0:T(1024)(128)(4,1)}), s8[4194304]{0:T(1024)(128)(4,1)S(1)}, s32[]{:S(2)}) async-start(s8[18874368]{0:T(1024)(128)(4,1)} %bitcast.39), calls=%async_computation.5 | async-start | bytes 8388608
  916.1 30.2 %slice-start.4 = ((s8[18874368]{0:T(1024)(128)(4,1)}), s8[4194304]{0:T(1024)(128)(4,1)S(1)}, s32[]{:S(2)}) async-start(s8[18874368]{0:T(1024)(128)(4,1)} %bitcast.39), calls=%async_computation.6 | async-start | bytes 8388608
  916.1 30.2 %slice-start.5 = ((s8[18874368]{0:T(1024)(128)(4,1)}), s8[2097152]{0:T(1024)(128)(4,1)S(1)}, s32[]{:S(2)}) async-start(s8[18874368]{0:T(1024)(128)(4,1)} %bitcast.39), calls=%async_computation.7 | async-start | bytes 4194304
  1039.2 3.7 copy-start.6
  (14 other events, 19.6 us)
Sparse Core Ops, SparseCore 0:
  39.4 544.5 all-reduce.8
  1039.3 1051.2 all-reduce.10
where the time goes:
time: 2110 us
  waiting for transfers between devices  1580 us (75%)
  local copies, waits for them, and re-layouts  401 us (19%)
  matrix products  88.8 us (4%)
  other arithmetic  26.5 us (1%)
    unnamed x4, waiting for transfers between devices  1580 us
    unnamed x76, local copies, waits for them, and re-layouts  94 us
    reshape x1, local copies, waits for them, and re-layouts, pack_whole(): jnp.concatenate([segment.reshape(shards, -1) for segment in pieces], axis=1)  85.6 us
    reshape x5, local copies, waits for them, and re-layouts, pack_whole(): segment.reshape(shards, -1)  72.3 us
    reshape x1, local copies, waits for them, and re-layouts, unpack_whole(): table = vector.reshape(shards, -1)  72.1 us
  transfers between devices with their start and end apart: 2, of which 2 were waited for; matrix products, arithmetic and copies ran while one was open for 1% of the time, Pallas kernels for 0%

commit v1 on v0

v1 whole, which is shorter than its diff:
```python
import jax
import jax.numpy as jnp
from jax import lax
from jax.sharding import PartitionSpec as P

D = 1024
FF = 4608
STEP = 10
AXES = ("rep", "zero")
TEAM = 4
DQ = D // TEAM
FQ = FF // TEAM
SMALL = 5
PAD = 128

norm_epsilon = 1e-05
first_decay = 0.9
second_decay = 0.999
moment_epsilon = 1e-08
weight_decay = 0.1
learn_rate = 0.06


def rms_scale(values):
    return lax.rsqrt(jnp.mean(values * values, axis=-1, keepdims=True) + norm_epsilon)


def shift_down(values, steps):
    return jnp.pad(values, ((steps, 0), (0, 0)))[: values.shape[0]]


def shift_up(values, steps):
    return jnp.pad(values, ((0, steps), (0, 0)))[steps:]


def matmul(left, right):
    return jnp.dot(left, right, preferred_element_type=jnp.float32)


def over_rows(left, right):
    return lax.dot_general(
        left, right, (((0,), (0,)), ((), ())), preferred_element_type=jnp.float32
    )


def against(left, right):
    return lax.dot_general(
        left, right, (((1,), (1,)), ((), ())), preferred_element_type=jnp.float32
    )


def slot_masks(seq_len, seq_dev, seq_off, owners, slots):
    index = jnp.arange(slots, dtype=jnp.int32)[None, :, None]
    mine = seq_dev[None, None, :] == owners[:, None, None]
    start = seq_off[None, None, :]
    covers = mine & (index >= start) & (index < start + seq_len[None, None, :])
    live = jnp.any(covers, axis=-1)
    opening = jnp.sum(jnp.where(covers, start, 0), axis=-1)
    position = index[:, :, 0] - opening
    column = lambda flags: flags.astype(jnp.float32).reshape(-1, 1)
    return column(live), column(live & (position >= 1)), column(live & (position >= 2))


def local(tokens, cotangent, seq_len, seq_dev, seq_off, params, first_moment, second_moment):
    shards = lax.axis_size(AXES)
    line = lax.axis_size("zero")
    device = lax.axis_index(AXES)
    ring = shards // TEAM
    quarter = device // ring
    slots = tokens.shape[0]
    rings = [[q * ring + w for w in range(ring)] for q in range(TEAM)]
    peers = [quarter ^ j for j in range(TEAM)]

    def send(value, flip):
        return lax.ppermute(value, AXES, [(k, k ^ flip) for k in range(shards)])

    def spread(value):
        return [value] + [send(value, j * ring) for j in range(1, TEAM)]

    def swap(blocks):
        return [blocks[0]] + [send(blocks[j], j * ring) for j in range(1, TEAM)]

    def in_order(pieces):
        odd, high = quarter % 2 == 1, quarter // 2 == 1
        low = [jnp.where(odd, pieces[i ^ 1], pieces[i]) for i in range(TEAM)]
        return jnp.stack([jnp.where(high, low[i ^ 2], low[i]) for i in range(TEAM)])

    def take(table, index, axis):
        return lax.dynamic_index_in_dim(table, index, axis=axis, keepdims=False)

    def pick(table, axis):
        return [take(table, peer, axis) for peer in peers]

    def after(value, earlier):
        return lax.optimization_barrier((value, earlier))

    def ring_gather(value, axis):
        return lax.all_gather(value, AXES, axis=axis, tiled=True, axis_index_groups=rings)

    core_flips = [ring >> i for i in range(1, ring.bit_length()) if ring >> i >= line]
    line_flips = [1 << i for i in range(line.bit_length() - 1)]

    def fold(value, axis, flips):
        for flip in flips:
            shape = value.shape
            half = shape[axis] // 2
            cut, place = ((2, half), axis) if flip >= line else ((half, 2), axis + 1)
            value = value.reshape(shape[:axis] + cut + shape[axis + 1 :])
            bit = (device // flip) % 2
            other = send(take(value, 1 - bit, place), flip)
            value = take(value, bit, place).astype(jnp.float32) + other.astype(jnp.float32)
            value = value.astype(jnp.bfloat16)
        return value

    rows = D // shards
    sizes = (rows * 3 * D, rows * D, rows * 2 * FF, FF // shards * D, SMALL * rows)
    starts = [sum(sizes[:i]) for i in range(6)]
    share = [params[starts[i] : starts[i + 1]] for i in range(5)]
    low = [part.astype(jnp.bfloat16) for part in share]

    deep = FF // shards
    block_early = jnp.concatenate([low[3].reshape(deep, D), low[1].reshape(rows, D)], axis=0)
    ring_early = ring_gather(block_early, 0).reshape(ring, deep + rows, D)

    block_small = jnp.pad(low[4].reshape(rows, SMALL), ((0, 0), (0, PAD - SMALL)))
    block_in = pick(low[0].reshape(rows, 3, TEAM, DQ), 2)
    block_in = [jnp.concatenate([b.reshape(rows, 3 * DQ), block_small], axis=1) for b in block_in]
    block_in = swap(block_in)
    block_in, own_tokens = after(block_in, tokens)
    token_parts = spread(own_tokens)
    block_in, ring_early = after(in_order(block_in), ring_early)
    ring_in = ring_gather(block_in, 1)

    token_parts, block_gu = after(token_parts, low[2])
    block_gu = pick(block_gu.reshape(rows, 2, TEAM, FQ), 2)
    block_gu = in_order(swap([b.reshape(rows, 2 * FQ) for b in block_gu]))
    weight_gateup = ring_gather(block_gu, 1).reshape(D, 2 * FQ)
    token_parts, late_cotangent = after(token_parts, cotangent)
    cotangent_parts = spread(late_cotangent)
    weight_down = ring_early[:, :deep].reshape(FQ, D)
    weight_out = ring_early[:, deep:].reshape(DQ, D)
    cotangent_parts, weight_out = after(cotangent_parts, weight_out)
    weight_out = spread(weight_out)
    weight_in = ring_in[:, :, : 3 * DQ].reshape(D, 3 * DQ)
    small = ring_in[:, :, 3 * DQ : 3 * DQ + SMALL].astype(jnp.float32).reshape(SMALL, D)
    gain_one = small[0]
    gain_two = small[1]
    taps = lax.dynamic_slice(small, (2, quarter * DQ), (3, DQ))

    owners = jnp.stack([peer * ring + device % ring for peer in peers])
    live, reach_one, reach_two = slot_masks(seq_len, seq_dev, seq_off, owners, slots)
    keeper = live[:slots]

    inputs = jnp.concatenate(token_parts, axis=0).astype(jnp.float32)
    unit_one = inputs * rms_scale(inputs)
    normed = (unit_one * gain_one).astype(jnp.bfloat16)
    mixin = matmul(normed, weight_in)
    b_part = mixin[:, :DQ]
    c_part = mixin[:, DQ : 2 * DQ]
    v_part = mixin[:, 2 * DQ :]
    product = b_part * v_part
    lag_one = shift_down(product, 1) * reach_one
    lag_two = shift_down(product, 2) * reach_two
    convolved = taps[0] * product + taps[1] * lag_one + taps[2] * lag_two
    gated = (c_part * convolved).astype(jnp.bfloat16)
    gated = swap([gated[j * slots : (j + 1) * slots] for j in range(TEAM)])

    own = tokens.astype(jnp.float32)
    own_scale = rms_scale(own)
    own_unit = own * own_scale
    branch = sum(matmul(gated[j], weight_out[j]) for j in range(TEAM))
    middle = own + keeper * branch
    scale_two = rms_scale(middle)
    unit_two = middle * scale_two
    normed_two = (unit_two * gain_two).astype(jnp.bfloat16)
    normed_two = spread(normed_two)

    upstream = jnp.concatenate(cotangent_parts, axis=0).astype(jnp.float32)
    feed_back = (live * upstream).astype(jnp.bfloat16)
    gate_up = matmul(jnp.concatenate(normed_two, axis=0), weight_gateup)
    gate_part = gate_up[:, :FQ]
    up_part = gate_up[:, FQ:]
    sigma = jax.nn.sigmoid(gate_part)
    swish = gate_part * sigma
    hidden = (swish * up_part).astype(jnp.bfloat16)
    hidden_back = against(feed_back, weight_down)
    gate_back = hidden_back * up_part * (sigma + gate_part * sigma * (1.0 - sigma))
    up_back = hidden_back * swish
    gateup_back = jnp.concatenate([gate_back, up_back], axis=1).astype(jnp.bfloat16)

    spans = [slice(j * slots, (j + 1) * slots) for j in range(TEAM)]
    normed_two_back = against(gateup_back, weight_gateup).astype(jnp.bfloat16)
    normed_two_back = [normed_two_back[span] for span in spans]
    normed_two_back, hidden = after(normed_two_back, hidden)
    normed_two_back = swap(normed_two_back)

    grad_down = over_rows(hidden, feed_back).astype(jnp.bfloat16)
    grad_down = fold(grad_down.reshape(ring, deep, D), 0, core_flips)
    early, (normed_two, hidden) = after(normed_two_back[1:3], (normed_two, hidden))
    feed_out = matmul(hidden, weight_down).astype(jnp.bfloat16)
    grad_gate = over_rows(jnp.concatenate(normed_two, axis=0), gateup_back[:, :FQ]).astype(jnp.bfloat16)
    grad_gate = fold(grad_gate.reshape(TEAM, ring, rows, FQ), 1, core_flips)
    grad_down = fold(grad_down, 0, line_flips[:1])
    normed_two_back = [normed_two_back[0], early[0], early[1], normed_two_back[3]]
    normed_two_back, (grad_down, grad_gate, feed_out) = after(
        normed_two_back, (grad_down, grad_gate, feed_out)
    )
    grad_down = fold(grad_down, 0, line_flips[1:])
    grad_gate = fold(grad_gate, 1, line_flips[:1])
    normed_two_back = sum(part.astype(jnp.float32) for part in normed_two_back)

    grad_gain_two = jnp.sum(normed_two_back * unit_two, axis=0)
    unit_two_back = normed_two_back * gain_two
    own_back = cotangent.astype(jnp.float32)
    middle_back = own_back + scale_two * (
        unit_two_back - unit_two * jnp.mean(unit_two_back * unit_two, axis=-1, keepdims=True)
    )
    branch_back = (keeper * middle_back).astype(jnp.bfloat16)
    gated_back = [against(branch_back, weight_out[j]).astype(jnp.bfloat16) for j in range(TEAM)]
    gated_back = swap(gated_back)
    gated_back[1], (gated, branch_back, normed_two) = after(
        gated_back[1], (gated, branch_back, normed_two)
    )
    grad_up = over_rows(jnp.concatenate(normed_two, axis=0), gateup_back[:, FQ:]).astype(jnp.bfloat16)
    grad_out = [over_rows(gated[j], branch_back).astype(jnp.bfloat16) for j in range(TEAM)]
    grad_out = swap(grad_out)
    gated_back, (grad_down, grad_gate) = after(gated_back, (grad_down, grad_gate))
    gated_back = jnp.concatenate(gated_back, axis=0).astype(jnp.float32)
    grad_up = fold(grad_up.reshape(TEAM, ring, rows, FQ), 1, core_flips)
    grad_gate = fold(grad_gate, 1, line_flips[1:])

    conv_back = gated_back * c_part
    c_back = gated_back * convolved
    grad_taps = jnp.stack(
        [
            jnp.sum(conv_back * product, axis=0),
            jnp.sum(conv_back * lag_one, axis=0),
            jnp.sum(conv_back * lag_two, axis=0),
        ]
    )
    product_back = (
        taps[0] * conv_back
        + shift_up(taps[1] * conv_back * reach_one, 1)
        + shift_up(taps[2] * conv_back * reach_two, 2)
    )
    mixin_back = jnp.concatenate(
        [product_back * v_part, c_back, product_back * b_part], axis=1
    ).astype(jnp.bfloat16)
    normed_back = against(mixin_back, weight_in)
    grad_gain_one = jnp.sum(normed_back * unit_one, axis=0)
    normed_back = normed_back.astype(jnp.bfloat16)
    normed_back = [jnp.concatenate([normed_back[span], feed_out[span]], axis=0) for span in spans]
    normed_back, (grad_gate, grad_up) = after(normed_back, (grad_gate, grad_up))
    normed_back = swap(normed_back)
    grad_out = sum(part.astype(jnp.float32) for part in grad_out).astype(jnp.bfloat16)
    grad_up = fold(grad_up, 1, line_flips[:1])
    small_terms = lax.dynamic_update_slice(
        jnp.zeros((SMALL, D), jnp.float32), grad_taps, (2, quarter * DQ)
    )
    small_terms = small_terms.at[0].set(grad_gain_one).at[1].set(grad_gain_two)
    small_terms = jnp.pad(small_terms.reshape(D, SMALL), ((0, 0), (0, PAD - SMALL)))
    grad_tail = [
        over_rows(normed, mixin_back).astype(jnp.bfloat16).reshape(TEAM, ring, rows, 3 * DQ),
        small_terms.astype(jnp.bfloat16).reshape(TEAM, ring, rows, PAD),
        grad_out.reshape(ring, rows, TEAM, DQ).transpose(2, 0, 1, 3),
    ]
    grad_tail = jnp.concatenate(grad_tail, axis=3)
    grad_tail = fold(grad_tail, 1, core_flips)
    grad_up = fold(grad_up, 1, line_flips[1:])
    grad_tail = fold(grad_tail, 1, line_flips[:1])
    grad_tail, normed_back, grad_up = lax.optimization_barrier((grad_tail, normed_back, grad_up))
    grad_tail = fold(grad_tail, 1, line_flips[1:]).reshape(TEAM, rows, 4 * DQ + PAD)
    normed_back = sum(part.astype(jnp.float32) for part in normed_back)
    normed_back, feed_out = normed_back[:slots], normed_back[slots:]
    mixed = (middle + keeper * feed_out).astype(jnp.bfloat16)
    unit_one_back = normed_back * gain_one
    inputs_back = middle_back + own_scale * (
        unit_one_back - own_unit * jnp.mean(unit_one_back * own_unit, axis=-1, keepdims=True)
    )
    token_grad = inputs_back.astype(jnp.bfloat16)

    split = 3 * DQ + PAD
    grad_out = grad_tail[:, :, split:].transpose(1, 0, 2).astype(jnp.float32).reshape(-1)
    grad_last = [grad_tail[:, :, :split], grad_gate.reshape(TEAM, rows, FQ)]
    grad_last = jnp.concatenate(grad_last + [grad_up.reshape(TEAM, rows, FQ)], axis=2)
    grad_last = swap(pick(grad_last, 0))
    small_grad = sum(part[:, 3 * DQ : 3 * DQ + SMALL].astype(jnp.float32) for part in grad_last)
    small_grad = small_grad.reshape(-1)

    def columns(parts, groups, width):
        ordered = in_order(parts).astype(jnp.float32).reshape(TEAM, rows, groups, width)
        return ordered.transpose(1, 2, 0, 3).reshape(-1)

    param_grad = jnp.concatenate(
        [
            columns([part[:, : 3 * DQ] for part in grad_last], 3, DQ),
            grad_out,
            columns([part[:, split:] for part in grad_last], 2, FQ),
            grad_down.astype(jnp.float32).reshape(-1),
            small_grad,
        ]
    )
    shard_len = params.shape[0]
    matrix_mask = (jnp.arange(shard_len) < starts[4]).astype(jnp.float32)
    moment = first_decay * first_moment + (1.0 - first_decay) * param_grad
    second_new = second_decay * second_moment + (1.0 - second_decay) * param_grad * param_grad
    moment_hat = moment / (1.0 - first_decay**STEP)
    second_hat = second_new / (1.0 - second_decay**STEP)
    params_new = params - learn_rate * (
        moment_hat / (jnp.sqrt(second_hat) + moment_epsilon) + weight_decay * matrix_mask * params
    )
    return (mixed, token_grad, param_grad, small_grad, second_new, params_new)


def solution(mesh):
    placed = (
        P(AXES, None),
        P(AXES, None),
        P(),
        P(),
        P(),
        P(AXES),
        P(AXES),
        P(AXES),
    )
    return jax.shard_map(
        local,
        mesh=mesh,
        in_specs=placed,
        out_specs=(P(AXES, None), P(AXES, None), P(AXES), P(AXES), P(AXES), P(AXES)),
        check_vma=False,
    )
```

time: 2110 us -> 406 us (0.19)
  waiting for transfers between devices: 1580 us -> 187 us
  local copies, waits for them, and re-layouts: 401 us -> 40.8 us
  starting transfers between devices: 0.08 us -> 53.7 us
  matrix products: 88.8 us -> 61.3 us
    unnamed x4 -> x3, waiting for transfers between devices: 1580 us -> 0.05 us
    reshape x7 -> x9, local copies, waits for them, and re-layouts: 230 us -> 4.14 us  [the longest x2 1.52 us: local(): grad_out.reshape(ring, rows, TEAM, DQ).transpose(2, 0, 1, 3)]
    ppermute x0 -> x48, waiting for transfers between devices: none -> 160 us  [send(): return lax.ppermute(value, AXES, [(k, k ^ flip) for k in range(shards)])]
    unnamed x76 -> x196, local copies, waits for them, and re-layouts: 94 us -> 13.2 us
    ppermute x0 -> x48, starting transfers between devices: none -> 53.6 us  [send(): return lax.ppermute(value, AXES, [(k, k ^ flip) for k in range(shards)])]
    another operation x8, local copies, waits for them, and re-layouts: 46.3 us -> 0.32 us  [in_order(): return jnp.stack([jnp.where(high, low[i ^ 2], low[i]) for i in range(TEAM)])]
    all_gather x0 -> x3, waiting for transfers between devices: none -> 26.9 us  [ring_gather(): lax.all_gather(value, AXES, axis=axis, tiled=True, axis_index_groups=rings)]
  transfers between devices with their start and end apart: 2 -> 51, of which waited for: 2 -> 26; matrix products, arithmetic and copies ran while one was open for 1% -> 22% of each run, Pallas kernels for 0% -> 0%
where the time goes in v1:
time: 406 us; the launch traced here: 398 us
  waiting for transfers between devices  187 us (46%)
  matrix products  61.3 us (15%)
  starting transfers between devices  53.7 us (13%)
  local copies, waits for them, and re-layouts  40.8 us (10%)
  other arithmetic  38.8 us (10%)
  between operations  15.9 us (4%)
    ppermute x48, waiting for transfers between devices, send(): return lax.ppermute(value, AXES, [(k, k ^ flip) for k in range(shards)])  160 us
    ppermute x48, starting transfers between devices, send(): return lax.ppermute(value, AXES, [(k, k ^ flip) for k in range(shards)])  53.6 us
    all_gather x3, waiting for transfers between devices, ring_gather(): lax.all_gather(value, AXES, axis=axis, tiled=True, axis_index_groups=rings)  26.9 us
    dot_general x8, matrix products, over_rows(): lax.dot_general(left, right, (((0,), (0,)), ((), ())), preferred_element_...  23.7 us
    dot_general x7, matrix products, against(): lax.dot_general(left, right, (((1,), (1,)), ((), ())), preferred_element_...  20.5 us
    dot_general x7, matrix products, matmul(): return jnp.dot(left, right, preferred_element_type=jnp.float32)  17 us
    unnamed x196, local copies, waits for them, and re-layouts  13.2 us
  transfers between devices with their start and end apart: 51, of which 26 were waited for; matrix products, arithmetic and copies ran while one was open for 22% of the time, Pallas kernels for 0%

profile of v1, /device:TPU:0, one launch (start us, length us, event | category | flops | bytes accessed | tf_op | source)
XLA Modules:
  0.0 397.9 jit_solution(15697086232174160087)
XLA Ops:
  22.2 26.9 %all-gather.4.cloned.1.call-done = bf16[1408,1024]{1,0:T(8,128)(2,1)} async-done(((bf16[176,1024]{1,0:T(8,128)(2,1)}), bf16[1408,1024]{1,0:T(8,128)(2,1)}) %all-gather.4.cloned.1.call-update) | async-done | bytes 2883600 | tf_op jit(solution)/shard_map/all_gather | solution.py:98
  52.7 11.2 %collective-permute-done.3 = bf16[256,1024]{1,0:T(8,128)(2,1)S(1)} collective-permute-done((bf16[256,1024]{1,0:T(8,128)(2,1)S(1)}, bf16[256,1024]{1,0:T(8,128)(2,1)S(1)}, u32[]{:S(2)}, u32[]{:S(2)}) %collective-permute-start.3) | collective-permute-done | bytes 524320 | tf_op jit(solution)/shard_map/ppermute | solution.py:75
  63.9 11.7 %collective-permute-done.4 = bf16[256,1024]{1,0:T(8,128)(2,1)S(1)} collective-permute-done((bf16[256,1024]{1,0:T(8,128)(2,1)S(1)}, bf16[256,1024]{1,0:T(8,128)(2,1)S(1)}, u32[]{:S(2)}, u32[]{:S(2)}) %collective-permute-start.4) | collective-permute-done | bytes 524320 | tf_op jit(solution)/shard_map/ppermute | solution.py:75
  75.9 4.0 %dynamic-slice_reduce_fusion.1 = (bf16[32,2,1152]{2,1,0:T(2,128)(2,1)S(1)}, bf16[32,2,1152]{2,1,0:T(2,128)(2,1)S(1)}, bf16[32,2,1152]{2,1,0:T(2,128)(2,1)S(1)}, bf16[32,2,1152]{2,1,0:T(2,128)(2,1)S(1)}) fusion(bf16[32,2,4,1152]{3,2,1,0:T(4,128)(2,1)S(1)} %reshape.441, s32[]{:T(128)S(6)} %select_n.301, s32[]{:T(128)S(6)} %select_n.300, s32[]{:T(128)S(6)} %select_n.302, ...), kind=kLoop, calls=%fused_computation.161 | loop fusion | bytes 1179664 | tf_op jit(solution)/shard_map/jit(dynamic_index_in_dim)/dynamic_slice | solution.py:89
  97.8 8.0 %collective-permute-done.6 = bf16[256,1024]{1,0:T(8,128)(2,1)S(1)} collective-permute-done((bf16[256,1024]{1,0:T(8,128)(2,1)S(1)}, bf16[256,1024]{1,0:T(8,128)(2,1)S(1)}, u32[]{:S(2)}, u32[]{:S(2)}) %collective-permute-start.6) | collective-permute-done | bytes 524320 | tf_op jit(solution)/shard_map/ppermute | solution.py:75
  105.8 11.1 %collective-permute-done.7 = bf16[256,1024]{1,0:T(8,128)(2,1)} collective-permute-done((bf16[256,1024]{1,0:T(8,128)(2,1)S(1)}, bf16[256,1024]{1,0:T(8,128)(2,1)}, u32[]{:S(2)}, u32[]{:S(2)}) %collective-permute-start.7) | collective-permute-done | bytes 524320 | tf_op jit(solution)/shard_map/ppermute | solution.py:75
  122.0 4.3 %fusion.68 = f32[1024,768]{1,0:T(8,128)S(1)} fusion(bf16[1024,768]{1,0:T(8,128)(2,1)S(1)} %bitcast.206, f32[1024]{0:T(1024)S(1)} %bitcast.240, f32[1024]{0:T(1024)S(1)} %add_rsqrt_fusion, bf16[256,1024]{1,0:T(8,128)(2,1)} %collective-permute-done.5, bf16[256,1024]{1,0:T(8,128)(2,1)S(1)} %copy-done.52, bf16[256,1024]{1,0:T(8,128)(2,1)S(1)} %copy-done.48, ...), kind=kOutput, calls=%fused_computation.140 | convolution fusion | flops 1622147072 | bytes 6823936 | tf_op jit(solution)/shard_map/dot_general | solution.py:37
  135.8 12.0 %collective-permute-done.11 = bf16[256,256]{1,0:T(8,128)(2,1)S(1)} collective-permute-done((bf16[256,256]{1,0:T(8,128)(2,1)S(1)}, bf16[256,256]{1,0:T(8,128)(2,1)S(1)}, u32[]{:S(2)}, u32[]{:S(2)}) %collective-permute-start.11) | collective-permute-done | bytes 131104 | tf_op jit(solution)/shard_map/ppermute | solution.py:75
  157.7 6.9 %collective-permute-done.15 = bf16[256,1024]{1,0:T(8,128)(2,1)} collective-permute-done((bf16[256,1024]{1,0:T(8,128)(2,1)S(1)}, bf16[256,1024]{1,0:T(8,128)(2,1)}, u32[]{:S(2)}, u32[]{:S(2)}) %collective-permute-start.15) | collective-permute-done | bytes 524320 | tf_op jit(solution)/shard_map/ppermute | solution.py:75
  164.6 10.4 %collective-permute-done.16 = bf16[256,1024]{1,0:T(8,128)(2,1)} collective-permute-done((bf16[256,1024]{1,0:T(8,128)(2,1)S(1)}, bf16[256,1024]{1,0:T(8,128)(2,1)}, u32[]{:S(2)}, u32[]{:S(2)}) %collective-permute-start.16) | collective-permute-done | bytes 524320 | tf_op jit(solution)/shard_map/ppermute | solution.py:75
  175.1 8.0 %fusion.14 = f32[1024,2304]{1,0:T(8,128)S(1)} fusion(bf16[1024,2304]{1,0:T(8,128)(2,1)} %bitcast.262, bf16[256,1024]{1,0:T(8,128)(2,1)} %collective-permute-done.17, bf16[256,1024]{1,0:T(8,128)(2,1)} %collective-permute-done.16, bf16[256,1024]{1,0:T(8,128)(2,1)} %collective-permute-done.15, bf16[256,1024]{1,0:T(8,128)(2,1)S(1)} %multiply_convert_fusion.7), kind=kOutput, calls=%fused_computation.34 | convolution fusion | flops 4840226816 | bytes 16252928 | tf_op jit(solution)/shard_map/dot_general | solution.py:37
  183.2 7.8 %multiply_convert_fusion.2 = (bf16[1024,1152]{1,0:T(8,128)(2,1)}, bf16[1024,1152]{1,0:T(8,128)(2,1)}, bf16[1024,1152]{1,0:T(8,128)(2,1)}) fusion(f32[1024,2304]{1,0:T(8,128)S(1)} %fusion.14, bf16[1152,1024]{1,0:T(8,128)(2,1)S(1)} %bitcast.198, bf16[256,1024]{1,0:T(8,128)(2,1)} %collective-permute-done.8, bf16[256,1024]{1,0:T(8,128)(2,1)} %collective-permute-done.7, ...), kind=kOutput, calls=%fused_computation.10 | convolution fusion | flops 2442919936 | bytes 20975616 | tf_op jit(solution)/shard_map/dot_general | solution.py:47
  191.0 7.9 %fusion.36 = bf16[1024,1024]{1,0:T(8,128)(2,1)S(1)} fusion(bf16[1024,2304]{1,0:T(8,128)(2,1)S(1)} %bitcast.265, bf16[1024,1152]{1,0:T(8,128)(2,1)} %get-tuple-element.192, bf16[1024,1152]{1,0:T(8,128)(2,1)} %get-tuple-element.191), kind=kOutput, calls=%fused_computation.58 | convolution fusion | flops 4842323968 | bytes 11534336 | tf_op jit(solution)/shard_map/dot_general | solution.py:47
  202.3 4.0 convolution_convert_fusion.2
  212.4 5.2 %convolution_convert_fusion.1 = bf16[1024,1152]{1,0:T(8,128)(2,1)S(1)} fusion(bf16[1024,1152]{1,0:T(8,128)(2,1)} %get-tuple-element.191, bf16[256,1024]{1,0:T(8,128)(2,1)} %collective-permute-done.17, bf16[256,1024]{1,0:T(8,128)(2,1)} %collective-permute-done.16, bf16[256,1024]{1,0:T(8,128)(2,1)} %collective-permute-done.15, bf16[256,1024]{1,0:T(8,128)(2,1)} %copy-done.55), kind=kOutput, calls=%fused_computation.18 | convolution fusion | flops 2425487360 | bytes 6815744 | tf_op jit(solution)/shard_map/dot_general | solution.py:41
  226.4 11.3 %collective-permute-done.25 = bf16[2,144,1024]{2,1,0:T(8,128)(2,1)S(1)} collective-permute-done((bf16[2,144,1024]{2,1,0:T(8,128)(2,1)S(1)}, bf16[2,144,1024]{2,1,0:T(8,128)(2,1)S(1)}, u32[]{:S(2)}, u32[]{:S(2)}) %collective-permute-start.25) | collective-permute-done | bytes 589856 | tf_op jit(solution)/shard_map/ppermute | solution.py:75
  252.2 4.3 %convolution_convert_fusion = bf16[1024,1152]{1,0:T(8,128)(2,1)S(1)} fusion(bf16[1024,1152]{1,0:T(8,128)(2,1)S(1)} %copy-done.86, bf16[256,1024]{1,0:T(8,128)(2,1)} %collective-permute-done.17, bf16[256,1024]{1,0:T(8,128)(2,1)} %collective-permute-done.16, bf16[256,1024]{1,0:T(8,128)(2,1)} %collective-permute-done.15, bf16[256,1024]{1,0:T(8,128)(2,1)S(1)} %copy-done.56), kind=kOutput, calls=%fused_computation.17 | convolution fusion | flops 2425487360 | bytes 6815744 | tf_op jit(solution)/shard_map/dot_general | solution.py:41
  290.0 4.3 %convolution_convert_fusion.4 = bf16[1024,768]{1,0:T(8,128)(2,1)} fusion(bf16[1024,256]{1,0:T(8,128)(2,1)S(1)} %copy-done.45, bf16[1024,256]{1,0:T(8,128)(2,1)S(1)} %copy-done.41, bf16[1024,256]{1,0:T(8,128)(2,1)S(1)} %copy-done.43, f32[1024]{0:T(1024)S(1)} %bitcast.241, f32[1024]{0:T(1024)S(1)} %copy-done.77, ...), kind=kOutput, calls=%fused_computation.59 | convolution fusion | flops 1627652096 | bytes 5251072 | tf_op jit(solution)/shard_map/dot_general | solution.py:41
  308.9 10.1 %collective-permute-done.42 = bf16[4,2,32,1152]{3,2,0,1:T(8,128)(2,1)S(1)} collective-permute-done((bf16[4,2,32,1152]{3,2,0,1:T(8,128)(2,1)S(1)}, bf16[4,2,32,1152]{3,2,0,1:T(8,128)(2,1)S(1)}, u32[]{:S(2)}, u32[]{:S(2)}) %collective-permute-start.42) | collective-permute-done | bytes 589856 | tf_op jit(solution)/shard_map/ppermute | solution.py:75
  322.6 11.6 %collective-permute-done.43 = bf16[4,1,32,1152]{3,2,0,1:T(8,128)(2,1)S(1)} collective-permute-done((bf16[4,1,32,1152]{3,2,0,1:T(8,128)(2,1)S(1)}, bf16[4,1,32,1152]{3,2,0,1:T(8,128)(2,1)S(1)}, u32[]{:S(2)}, u32[]{:S(2)}) %collective-permute-start.43) | collective-permute-done | bytes 294944 | tf_op jit(solution)/shard_map/ppermute | solution.py:75
  334.3 6.7 %collective-permute-done.36 = bf16[4,2,32,1152]{3,2,1,0:T(8,128)(2,1)S(1)} collective-permute-done((bf16[4,2,32,1152]{3,2,1,0:T(8,128)(2,1)S(1)}, bf16[4,2,32,1152]{3,2,1,0:T(8,128)(2,1)S(1)}, u32[]{:S(2)}, u32[]{:S(2)}) %collective-permute-start.36) | collective-permute-done | bytes 589856 | tf_op jit(solution)/shard_map/ppermute | solution.py:75
  341.2 11.6 %collective-permute-done.40 = bf16[512,1024]{1,0:T(8,128)(2,1)S(1)} collective-permute-done((bf16[512,1024]{1,0:T(8,128)(2,1)S(1)}, bf16[512,1024]{1,0:T(8,128)(2,1)S(1)}, u32[]{:S(2)}, u32[]{:S(2)}) %collective-permute-start.40) | collective-permute-done | bytes 1048608 | tf_op jit(solution)/shard_map/ppermute | solution.py:75
  357.8 9.7 %collective-permute-done.44 = bf16[4,1,32,1152]{3,2,1,0:T(8,128)(2,1)S(1)} collective-permute-done((bf16[4,1,32,1152]{3,2,1,0:T(8,128)(2,1)S(1)}, bf16[4,1,32,1152]{3,2,1,0:T(8,128)(2,1)S(1)}, u32[]{:S(2)}, u32[]{:S(2)}) %collective-permute-start.44) | collective-permute-done | bytes 294944 | tf_op jit(solution)/shard_map/ppermute | solution.py:75
  372.1 4.6 %collective-permute-done.45 = bf16[32,3200]{1,0:T(8,128)(2,1)S(1)} collective-permute-done((bf16[32,3200]{1,0:T(8,128)(2,1)S(1)}, bf16[32,3200]{1,0:T(8,128)(2,1)S(1)}, u32[]{:S(2)}, u32[]{:S(2)}) %collective-permute-start.45) | collective-permute-done | bytes 204832 | tf_op jit(solution)/shard_map/ppermute | solution.py:75
  (421 shorter events, 168.4 us)
Async XLA Ops:
  7.2 41.9 %all-gather.4.cloned.1.call-start = ((), (), s32[]{:S(2)}) async-start(), calls=%async_computation | async-start | bytes 3244032 | tf_op jit(solution)/shard_map/all_gather | solution.py:98
  10.0 108.9 %all-gather.6.cloned.1.call-start = ((), (), s32[]{:S(2)}) async-start(), calls=%async_computation.1 | async-start | bytes 2064384 | tf_op jit(solution)/shard_map/all_gather | solution.py:98
  49.1 126.0 %all-gather.8.cloned.1.call-start = ((), (), s32[]{:S(2)}) async-start(), calls=%async_computation.2 | async-start | bytes 5308416 | tf_op jit(solution)/shard_map/all_gather | solution.py:98
  50.6 25.0 %collective-permute-start.4 = (bf16[256,1024]{1,0:T(8,128)(2,1)S(1)}, bf16[256,1024]{1,0:T(8,128)(2,1)S(1)}, u32[]{:S(2)}, u32[]{:S(2)}) collective-permute-start(bf16[256,1024]{1,0:T(8,128)(2,1)S(1)} %copy-done), channel_id=1, source_target_pairs={{0,16},{1,17},{2,18},{3,19},{4,20},{5,21},{6,22},{7,23},{8,24},{9,... | collective-permute-start | bytes 1572872 | tf_op jit(solution)/shard_map/ppermute | solution.py:75
  52.1 23.6 %collective-permute-start.5 = (bf16[256,1024]{1,0:T(8,128)(2,1)S(1)}, bf16[256,1024]{1,0:T(8,128)(2,1)}, u32[]{:S(2)}, u32[]{:S(2)}) collective-permute-start(bf16[256,1024]{1,0:T(8,128)(2,1)S(1)} %copy-done), channel_id=1, source_target_pairs={{0,24},{1,25},{2,26},{3,27},{4,28},{5,29},{6,30},{7,31},{8,16},{9,... | collective-permute-start | bytes 1572872 | tf_op jit(solution)/shard_map/ppermute | solution.py:75
  92.4 24.5 %collective-permute-start.7 = (bf16[256,1024]{1,0:T(8,128)(2,1)S(1)}, bf16[256,1024]{1,0:T(8,128)(2,1)}, u32[]{:S(2)}, u32[]{:S(2)}) collective-permute-start(bf16[256,1024]{1,0:T(8,128)(2,1)S(1)} %copy-done.37), channel_id=1, source_target_pairs={{0,16},{1,17},{2,18},{3,19},{4,20},{5,21},{6,22},{7,23},{8,24},{9,... | collective-permute-start | bytes 1572872 | tf_op jit(solution)/shard_map/ppermute | solution.py:75
  93.0 24.0 %collective-permute-start.8 = (bf16[256,1024]{1,0:T(8,128)(2,1)S(1)}, bf16[256,1024]{1,0:T(8,128)(2,1)}, u32[]{:S(2)}, u32[]{:S(2)}) collective-permute-start(bf16[256,1024]{1,0:T(8,128)(2,1)S(1)} %copy-done.37), channel_id=1, source_target_pairs={{0,24},{1,25},{2,26},{3,27},{4,28},{5,29},{6,30},{7,31},{8,16},{9,... | collective-permute-start | bytes 1572872 | tf_op jit(solution)/shard_map/ppermute | solution.py:75
  129.6 18.5 %collective-permute-start.14 = (bf16[256,1024]{1,0:T(8,128)(2,1)S(1)}, bf16[256,1024]{1,0:T(8,128)(2,1)S(1)}, u32[]{:S(2)}, u32[]{:S(2)}) collective-permute-start(bf16[256,1024]{1,0:T(8,128)(2,1)S(1)} %bitcast.185), channel_id=1, source_target_pairs={{0,24},{1,25},{2,26},{3,27},{4,28},{5,29},{6,30},{7,31},{8,16},{9,... | collective-permute-start | bytes 1572872 | tf_op jit(solution)/shard_map/ppermute | solution.py:75
  151.1 23.9 %collective-permute-start.16 = (bf16[256,1024]{1,0:T(8,128)(2,1)S(1)}, bf16[256,1024]{1,0:T(8,128)(2,1)}, u32[]{:S(2)}, u32[]{:S(2)}) collective-permute-start(bf16[256,1024]{1,0:T(8,128)(2,1)S(1)} %multiply_convert_fusion.7), channel_id=1, source_target_pairs={{0,16},{1,17},{2,18},{3,19},{4,20},{5,21},{6,22},{7,23},{8,24},{9,... | collective-permute-start | bytes 1572872 | tf_op jit(solution)/shard_map/ppermute | solution.py:75
  151.7 23.4 %collective-permute-start.17 = (bf16[256,1024]{1,0:T(8,128)(2,1)S(1)}, bf16[256,1024]{1,0:T(8,128)(2,1)}, u32[]{:S(2)}, u32[]{:S(2)}) collective-permute-start(bf16[256,1024]{1,0:T(8,128)(2,1)S(1)} %multiply_convert_fusion.7), channel_id=1, source_target_pairs={{0,24},{1,25},{2,26},{3,27},{4,28},{5,29},{6,30},{7,31},{8,16},{9,... | collective-permute-start | bytes 1572872 | tf_op jit(solution)/shard_map/ppermute | solution.py:75
  218.7 19.2 %collective-permute-start.23 = (bf16[256,1024]{1,0:T(8,128)(2,1)S(1)}, bf16[256,1024]{1,0:T(8,128)(2,1)S(1)}, u32[]{:S(2)}, u32[]{:S(2)}) collective-permute-start(bf16[256,1024]{1,0:T(8,128)(2,1)S(1)} %copy-done.57), channel_id=1, source_target_pairs={{0,24},{1,25},{2,26},{3,27},{4,28},{5,29},{6,30},{7,31},{8,16},{9,... | collective-permute-start | bytes 1572872 | tf_op jit(solution)/shard_map/ppermute | solution.py:75
  245.4 21.0 %collective-permute-start.31 = (bf16[4,2,32,1152]{3,2,0,1:T(8,128)(2,1)S(1)}, bf16[4,2,32,1152]{3,2,0,1:T(8,128)(2,1)S(1)}, u32[]{:S(2)}, u32[]{:S(2)}) collective-permute-start(bf16[4,2,32,1152]{3,2,0,1:T(8,128)(2,1)S(1)} %bitcast.214), channel_id=1, source_target_pairs={{0,1},{1,0},{2,3},{3,2},{4,5},{5,4},{6,7},{7,6},{8,9},{9,8},{10,11... | collective-permute-start | bytes 1769480 | tf_op jit(solution)/shard_map/ppermute | solution.py:75
  245.8 18.4 %collective-permute-start.30 = (bf16[1,144,1024]{2,1,0:T(8,128)(2,1)S(1)}, bf16[1,144,1024]{2,1,0:T(8,128)(2,1)S(1)}, u32[]{:S(2)}, u32[]{:S(2)}) collective-permute-start(bf16[1,144,1024]{2,1,0:T(8,128)(2,1)S(1)} %constant_dynamic-slice_fusion.7), channel_id=1, source_target_pairs={{0,2},{1,3},{2,0},{3,1},{4,6},{5,7},{6,4},{7,5},{8,10},{9,11},{10,... | collective-permute-start | bytes 884744 | tf_op jit(solution)/shard_map/ppermute | solution.py:75
  247.7 19.2 %collective-permute-start.29 = (bf16[256,256]{1,0:T(8,128)(2,1)S(1)}, bf16[256,256]{1,0:T(8,128)(2,1)S(1)}, u32[]{:S(2)}, u32[]{:S(2)}) collective-permute-start(bf16[256,256]{1,0:T(8,128)(2,1)S(1)} %convolution_convert_fusion.9), channel_id=1, source_target_pairs={{0,24},{1,25},{2,26},{3,27},{4,28},{5,29},{6,30},{7,31},{8,16},{9,... | collective-permute-start | bytes 393224 | tf_op jit(solution)/shard_map/ppermute | solution.py:75
  249.5 18.9 %collective-permute-start.28 = (bf16[256,256]{1,0:T(8,128)(2,1)S(1)}, bf16[256,256]{1,0:T(8,128)(2,1)S(1)}, u32[]{:S(2)}, u32[]{:S(2)}) collective-permute-start(bf16[256,256]{1,0:T(8,128)(2,1)S(1)} %convolution_convert_fusion.10), channel_id=1, source_target_pairs={{0,16},{1,17},{2,18},{3,19},{4,20},{5,21},{6,22},{7,23},{8,24},{9,... | collective-permute-start | bytes 393224 | tf_op jit(solution)/shard_map/ppermute | solution.py:75
  257.8 44.5 %collective-permute-start.38 = (bf16[4,4,32,1152]{3,2,1,0:T(8,128)(2,1)}, bf16[4,4,32,1152]{3,2,1,0:T(8,128)(2,1)}, u32[]{:S(2)}, u32[]{:S(2)}) collective-permute-start(bf16[4,4,32,1152]{3,2,1,0:T(8,128)(2,1)} %dynamic-slice_bitcast_fusion), channel_id=1, source_target_pairs={{0,4},{1,5},{2,6},{3,7},{4,0},{5,1},{6,2},{7,3},{8,12},{9,13},{10,... | collective-permute-start | bytes 3538952 | tf_op jit(solution)/shard_map/ppermute | solution.py:75
  264.2 30.1 %collective-permute-start.32 = (bf16[256,1024]{1,0:T(8,128)(2,1)}, bf16[256,1024]{1,0:T(8,128)(2,1)}, u32[]{:S(2)}, u32[]{:S(2)}) collective-permute-start(bf16[256,1024]{1,0:T(8,128)(2,1)} %convolution_convert_fusion.7), channel_id=1, source_target_pairs={{0,8},{1,9},{2,10},{3,11},{4,12},{5,13},{6,14},{7,15},{8,0},{9,1},... | collective-permute-start | bytes 1572872 | tf_op jit(solution)/shard_map/ppermute | solution.py:75
  266.4 27.9 %collective-permute-start.33 = (bf16[256,1024]{1,0:T(8,128)(2,1)}, bf16[256,1024]{1,0:T(8,128)(2,1)}, u32[]{:S(2)}, u32[]{:S(2)}) collective-permute-start(bf16[256,1024]{1,0:T(8,128)(2,1)} %convolution_convert_fusion.6), channel_id=1, source_target_pairs={{0,16},{1,17},{2,18},{3,19},{4,20},{5,21},{6,22},{7,23},{8,24},{9,... | collective-permute-start | bytes 1572872 | tf_op jit(solution)/shard_map/ppermute | solution.py:75
  266.9 27.3 %collective-permute-start.34 = (bf16[256,1024]{1,0:T(8,128)(2,1)}, bf16[256,1024]{1,0:T(8,128)(2,1)}, u32[]{:S(2)}, u32[]{:S(2)}) collective-permute-start(bf16[256,1024]{1,0:T(8,128)(2,1)} %convolution_convert_fusion.5), channel_id=1, source_target_pairs={{0,24},{1,25},{2,26},{3,27},{4,28},{5,29},{6,30},{7,31},{8,16},{9,... | collective-permute-start | bytes 1572872 | tf_op jit(solution)/shard_map/ppermute | solution.py:75
  269.2 31.2 %collective-permute-start.37 = (bf16[4,1,32,1152]{3,2,0,1:T(8,128)(2,1)}, bf16[4,1,32,1152]{3,2,0,1:T(8,128)(2,1)}, u32[]{:S(2)}, u32[]{:S(2)}) collective-permute-start(bf16[4,1,32,1152]{3,2,0,1:T(8,128)(2,1)} %constant_dynamic-slice_fusion.4), channel_id=1, source_target_pairs={{0,2},{1,3},{2,0},{3,1},{4,6},{5,7},{6,4},{7,5},{8,10},{9,11},{10,... | collective-permute-start | bytes 884744 | tf_op jit(solution)/shard_map/ppermute | solution.py:75
  305.1 36.0 %collective-permute-start.39 = (bf16[512,1024]{1,0:T(8,128)(2,1)S(1)}, bf16[512,1024]{1,0:T(8,128)(2,1)S(1)}, u32[]{:S(2)}, u32[]{:S(2)}) collective-permute-start(bf16[512,1024]{1,0:T(8,128)(2,1)S(1)} %copy-done.36), channel_id=1, source_target_pairs={{0,8},{1,9},{2,10},{3,11},{4,12},{5,13},{6,14},{7,15},{8,0},{9,1},... | collective-permute-start | bytes 3145736 | tf_op jit(solution)/shard_map/ppermute | solution.py:75
  305.8 46.9 %collective-permute-start.40 = (bf16[512,1024]{1,0:T(8,128)(2,1)S(1)}, bf16[512,1024]{1,0:T(8,128)(2,1)S(1)}, u32[]{:S(2)}, u32[]{:S(2)}) collective-permute-start(bf16[512,1024]{1,0:T(8,128)(2,1)S(1)} %copy-done.35), channel_id=1, source_target_pairs={{0,16},{1,17},{2,18},{3,19},{4,20},{5,21},{6,22},{7,23},{8,24},{9,... | collective-permute-start | bytes 3145736 | tf_op jit(solution)/shard_map/ppermute | solution.py:75
  306.8 45.9 %collective-permute-start.41 = (bf16[512,1024]{1,0:T(8,128)(2,1)S(1)}, bf16[512,1024]{1,0:T(8,128)(2,1)S(1)}, u32[]{:S(2)}, u32[]{:S(2)}) collective-permute-start(bf16[512,1024]{1,0:T(8,128)(2,1)S(1)} %copy-done.34), channel_id=1, source_target_pairs={{0,24},{1,25},{2,26},{3,27},{4,28},{5,29},{6,30},{7,31},{8,16},{9,... | collective-permute-start | bytes 3145736 | tf_op jit(solution)/shard_map/ppermute | solution.py:75
  320.6 20.4 %collective-permute-start.36 = (bf16[4,2,32,1152]{3,2,1,0:T(8,128)(2,1)S(1)}, bf16[4,2,32,1152]{3,2,1,0:T(8,128)(2,1)S(1)}, u32[]{:S(2)}, u32[]{:S(2)}) collective-permute-start(bf16[4,2,32,1152]{3,2,1,0:T(8,128)(2,1)S(1)} %dynamic-slice_bitcast_fusion.4), channel_id=1, source_target_pairs={{0,1},{1,0},{2,3},{3,2},{4,5},{5,4},{6,7},{7,6},{8,9},{9,8},{10,11... | collective-permute-start | bytes 1769480 | tf_op jit(solution)/shard_map/ppermute | solution.py:75
  (116 other events, 954.7 us)
Sparse Core Ops, SparseCore 0:
  10.2 38.8 all-gather.3
  51.2 25.7 all-gather.5
  90.3 49.6 all-gather.7

commit v2 on v1

--- a/solution.py
+++ b/solution.py
@@ -75,7 +75,24 @@
         return lax.ppermute(value, AXES, [(k, k ^ flip) for k in range(shards)])
 
     def spread(value):
-        return [value] + [send(value, j * ring) for j in range(1, TEAM)]
+        half = value.shape[0] // 2
+        beside, above = send(value, ring), send(value, 2 * ring)
+        across = [send(above[:half], ring), send(beside[half:], 2 * ring)]
+        return [value, beside, above, jnp.concatenate(across, axis=0)]
+
+    def shed(blocks):
+        half = blocks[3].shape[0] // 2
+        upper, lower = send(blocks[3][:half], ring), send(blocks[3][half:], 2 * ring)
+        wide = [block.astype(jnp.float32) for block in (blocks[1], blocks[2], upper, lower)]
+        beside = jnp.concatenate([wide[0][:half], wide[0][half:] + wide[3]], axis=0)
+        above = jnp.concatenate([wide[1][:half] + wide[2], wide[1][half:]], axis=0)
+        return blocks[0], beside.astype(jnp.bfloat16), above.astype(jnp.bfloat16)
+
+    def merge(own, beside, above):
+        return own, send(beside, ring), send(above, 2 * ring)
+
+    def total(parts):
+        return sum(part.astype(jnp.float32) for part in parts)
 
     def swap(blocks):
         return [blocks[0]] + [send(blocks[j], j * ring) for j in range(1, TEAM)]
@@ -119,27 +136,21 @@
     low = [part.astype(jnp.bfloat16) for part in share]
 
     deep = FF // shards
-    block_early = jnp.concatenate([low[3].reshape(deep, D), low[1].reshape(rows, D)], axis=0)
-    ring_early = ring_gather(block_early, 0).reshape(ring, deep + rows, D)
-
     block_small = jnp.pad(low[4].reshape(rows, SMALL), ((0, 0), (0, PAD - SMALL)))
     block_in = pick(low[0].reshape(rows, 3, TEAM, DQ), 2)
     block_in = [jnp.concatenate([b.reshape(rows, 3 * DQ), block_small], axis=1) for b in block_in]
     block_in = swap(block_in)
-    block_in, own_tokens = after(block_in, tokens)
+    block_in[1], own_tokens = after(block_in[1], tokens)
     token_parts = spread(own_tokens)
-    block_in, ring_early = after(in_order(block_in), ring_early)
-    ring_in = ring_gather(block_in, 1)
-
-    token_parts, block_gu = after(token_parts, low[2])
+    block_out = low[1].reshape(rows, TEAM, DQ).transpose(1, 0, 2)
+    ring_in = ring_gather(jnp.concatenate([in_order(block_in), block_out], axis=2), 1)
+
+    token_parts[1], (token_parts[2], block_gu) = after(token_parts[1], (token_parts[2], low[2]))
     block_gu = pick(block_gu.reshape(rows, 2, TEAM, FQ), 2)
     block_gu = in_order(swap([b.reshape(rows, 2 * FQ) for b in block_gu]))
     weight_gateup = ring_gather(block_gu, 1).reshape(D, 2 * FQ)
-    token_parts, late_cotangent = after(token_parts, cotangent)
-    cotangent_parts = spread(late_cotangent)
-    weight_down = ring_early[:, :deep].reshape(FQ, D)
-    weight_out = ring_early[:, deep:].reshape(DQ, D)
-    cotangent_parts, weight_out = after(cotangent_parts, weight_out)
+    weight_down = ring_gather(low[3].reshape(deep, D), 0)
+    weight_out = ring_in[:, :, 3 * DQ + PAD :].transpose(1, 0, 2).reshape(DQ, D)
     weight_out = spread(weight_out)
     weight_in = ring_in[:, :, : 3 * DQ].reshape(D, 3 * DQ)
     small = ring_in[:, :, 3 * DQ : 3 * DQ + SMALL].astype(jnp.float32).reshape(SMALL, D)
@@ -174,10 +185,13 @@
     unit_two = middle * scale_two
     normed_two = (unit_two * gain_two).astype(jnp.bfloat16)
     normed_two = spread(normed_two)
+    normed_two, late_cotangent = after(normed_two, cotangent)
+    cotangent_parts = spread(late_cotangent)
+    normed_two = jnp.concatenate(normed_two, axis=0)
 
     upstream = jnp.concatenate(cotangent_parts, axis=0).astype(jnp.float32)
     feed_back = (live * upstream).astype(jnp.bfloat16)
-    gate_up = matmul(jnp.concatenate(normed_two, axis=0), weight_gateup)
+    gate_up = matmul(normed_two, weight_gateup)
     gate_part = gate_up[:, :FQ]
     up_part = gate_up[:, FQ:]
     sigma = jax.nn.sigmoid(gate_part)
@@ -192,22 +206,15 @@
     normed_two_back = against(gateup_back, weight_gateup).astype(jnp.bfloat16)
     normed_two_back = [normed_two_back[span] for span in spans]
     normed_two_back, hidden = after(normed_two_back, hidden)
-    normed_two_back = swap(normed_two_back)
-
     grad_down = over_rows(hidden, feed_back).astype(jnp.bfloat16)
     grad_down = fold(grad_down.reshape(ring, deep, D), 0, core_flips)
-    early, (normed_two, hidden) = after(normed_two_back[1:3], (normed_two, hidden))
-    feed_out = matmul(hidden, weight_down).astype(jnp.bfloat16)
-    grad_gate = over_rows(jnp.concatenate(normed_two, axis=0), gateup_back[:, :FQ]).astype(jnp.bfloat16)
+    normed_two_back, normed_two = after(shed(normed_two_back), normed_two)
+    normed_two_back = merge(*normed_two_back)
+    grad_gate = over_rows(normed_two, gateup_back[:, :FQ]).astype(jnp.bfloat16)
     grad_gate = fold(grad_gate.reshape(TEAM, ring, rows, FQ), 1, core_flips)
+    normed_two_back, grad_down = after(normed_two_back, grad_down)
     grad_down = fold(grad_down, 0, line_flips[:1])
-    normed_two_back = [normed_two_back[0], early[0], early[1], normed_two_back[3]]
-    normed_two_back, (grad_down, grad_gate, feed_out) = after(
-        normed_two_back, (grad_down, grad_gate, feed_out)
-    )
-    grad_down = fold(grad_down, 0, line_flips[1:])
-    grad_gate = fold(grad_gate, 1, line_flips[:1])
-    normed_two_back = sum(part.astype(jnp.float32) for part in normed_two_back)
+    normed_two_back = total(normed_two_back)
 
     grad_gain_two = jnp.sum(normed_two_back * unit_two, axis=0)
     unit_two_back = normed_two_back * gain_two
@@ -217,17 +224,18 @@
     )
     branch_back = (keeper * middle_back).astype(jnp.bfloat16)
     gated_back = [against(branch_back, weight_out[j]).astype(jnp.bfloat16) for j in range(TEAM)]
+    gated_back, (gated, branch_back) = after(gated_back, (gated, branch_back))
     gated_back = swap(gated_back)
-    gated_back[1], (gated, branch_back, normed_two) = after(
-        gated_back[1], (gated, branch_back, normed_two)
-    )
-    grad_up = over_rows(jnp.concatenate(normed_two, axis=0), gateup_back[:, FQ:]).astype(jnp.bfloat16)
-    grad_out = [over_rows(gated[j], branch_back).astype(jnp.bfloat16) for j in range(TEAM)]
-    grad_out = swap(grad_out)
+    grad_out = shed([over_rows(gated[j], branch_back).astype(jnp.bfloat16) for j in range(TEAM)])
+    gated_back[1], (normed_two, hidden) = after(gated_back[1], (normed_two, hidden))
+    grad_up = over_rows(normed_two, gateup_back[:, FQ:]).astype(jnp.bfloat16)
+    grad_up = fold(grad_up.reshape(TEAM, ring, rows, FQ), 1, core_flips)
+    feed_out = matmul(hidden, weight_down).astype(jnp.bfloat16)
     gated_back, (grad_down, grad_gate) = after(gated_back, (grad_down, grad_gate))
     gated_back = jnp.concatenate(gated_back, axis=0).astype(jnp.float32)
-    grad_up = fold(grad_up.reshape(TEAM, ring, rows, FQ), 1, core_flips)
-    grad_gate = fold(grad_gate, 1, line_flips[1:])
+    grad_down = fold(grad_down, 0, line_flips[1:])
+    grad_gate = fold(grad_gate, 1, line_flips[:1])
+    grad_out = merge(*grad_out)
 
     conv_back = gated_back * c_part
     c_back = gated_back * convolved
@@ -249,11 +257,16 @@
     normed_back = against(mixin_back, weight_in)
     grad_gain_one = jnp.sum(normed_back * unit_one, axis=0)
     normed_back = normed_back.astype(jnp.bfloat16)
-    normed_back = [jnp.concatenate([normed_back[span], feed_out[span]], axis=0) for span in spans]
-    normed_back, (grad_gate, grad_up) = after(normed_back, (grad_gate, grad_up))
-    normed_back = swap(normed_back)
-    grad_out = sum(part.astype(jnp.float32) for part in grad_out).astype(jnp.bfloat16)
+    normed_back = shed([normed_back[span] for span in spans])
+    normed_back, (grad_down, grad_gate, grad_up) = after(
+        normed_back, (grad_down, grad_gate, grad_up)
+    )
+    grad_out = total(grad_out).astype(jnp.bfloat16)
+    normed_back = merge(*normed_back)
+    feed_out = shed([feed_out[span] for span in spans])
+    grad_gate = fold(grad_gate, 1, line_flips[1:])
     grad_up = fold(grad_up, 1, line_flips[:1])
+
     small_terms = lax.dynamic_update_slice(
         jnp.zeros((SMALL, D), jnp.float32), grad_taps, (2, quarter * DQ)
     )
@@ -266,13 +279,16 @@
     ]
     grad_tail = jnp.concatenate(grad_tail, axis=3)
     grad_tail = fold(grad_tail, 1, core_flips)
+    grad_tail, (grad_gate, grad_up) = after(grad_tail, (grad_gate, grad_up))
+    grad_tail = fold(grad_tail, 1, line_flips[:1])
     grad_up = fold(grad_up, 1, line_flips[1:])
-    grad_tail = fold(grad_tail, 1, line_flips[:1])
-    grad_tail, normed_back, grad_up = lax.optimization_barrier((grad_tail, normed_back, grad_up))
+    grad_tail, (grad_up, normed_back, feed_out) = after(
+        grad_tail, (grad_up, normed_back, feed_out)
+    )
     grad_tail = fold(grad_tail, 1, line_flips[1:]).reshape(TEAM, rows, 4 * DQ + PAD)
-    normed_back = sum(part.astype(jnp.float32) for part in normed_back)
-    normed_back, feed_out = normed_back[:slots], normed_back[slots:]
+    feed_out = total(merge(*feed_out))
     mixed = (middle + keeper * feed_out).astype(jnp.bfloat16)
+    normed_back = total(normed_back)
     unit_one_back = normed_back * gain_one
     inputs_back = middle_back + own_scale * (
         unit_one_back - own_unit * jnp.mean(unit_one_back * own_unit, axis=-1, keepdims=True)

time: 406 us -> 358 us (0.88)
  waiting for transfers between devices: 187 us -> 130 us
  starting transfers between devices: 53.7 us -> 64.1 us
  matrix products: 61.3 us -> 55.1 us
    ppermute x48 -> x59, waiting for transfers between devices: 160 us -> 130 us  [send(): return lax.ppermute(value, AXES, [(k, k ^ flip) for k in range(shards)])]
    all_gather x3, waiting for transfers between devices: 26.9 us -> 0.02 us  [ring_gather(): lax.all_gather(value, AXES, axis=axis, tiled=True, axis_index_groups=rings)]
    ppermute x48 -> x59, starting transfers between devices: 53.6 us -> 63.5 us  [send(): return lax.ppermute(value, AXES, [(k, k ^ flip) for k in range(shards)])]
    unnamed x196 -> x172, local copies, waits for them, and re-layouts: 13.2 us -> 18.4 us
    dot_general x8, matrix products: 23.7 us -> 18.6 us  [over_rows(): lax.dot_general(left, right, (((0,), (0,)), ((), ())), preferred_element_...]
  transfers between devices with their start and end apart: 51 -> 62, of which waited for: 26 -> 34; matrix products, arithmetic and copies ran while one was open for 22% -> 32% of each run, Pallas kernels for 0% -> 0%
where the time goes in v2:
time: 358 us; the launch traced here: 352 us
  waiting for transfers between devices  130 us (36%)
  starting transfers between devices  64.1 us (18%)
  matrix products  55.1 us (15%)
  local copies, waits for them, and re-layouts  44.6 us (12%)
  other arithmetic  41.8 us (12%)
  between operations  16.2 us (5%)
    ppermute x59, waiting for transfers between devices, send(): return lax.ppermute(value, AXES, [(k, k ^ flip) for k in range(shards)])  130 us
    ppermute x59, starting transfers between devices, send(): return lax.ppermute(value, AXES, [(k, k ^ flip) for k in range(shards)])  63.5 us
    dot_general x7, matrix products, matmul(): return jnp.dot(left, right, preferred_element_type=jnp.float32)  18.9 us
    dot_general x8, matrix products, over_rows(): lax.dot_general(left, right, (((0,), (0,)), ((), ())), preferred_element_...  18.6 us
    unnamed x172, local copies, waits for them, and re-layouts  18.4 us
    dot_general x7, matrix products, against(): lax.dot_general(left, right, (((1,), (1,)), ((), ())), preferred_element_...  17.6 us
    dynamic_slice x6, local copies, waits for them, and re-layouts, take(): return lax.dynamic_index_in_dim(table, index, axis=axis, keepdims=False)  7.31 us
  transfers between devices with their start and end apart: 62, of which 34 were waited for; matrix products, arithmetic and copies ran while one was open for 32% of the time, Pallas kernels for 0%

profile of v2, /device:TPU:0, one launch (start us, length us, event | category | flops | bytes accessed | tf_op | source)
XLA Modules:
  0.0 352.3 jit_solution(3465263062530075522)
XLA Ops:
  22.5 10.3 %collective-permute-done.1 = bf16[256,1024]{1,0:T(8,128)(2,1)S(1)} collective-permute-done((bf16[256,1024]{1,0:T(8,128)(2,1)S(1)}, bf16[256,1024]{1,0:T(8,128)(2,1)S(1)}, u32[]{:S(2)}, u32[]{:S(2)}) %collective-permute-start.1) | collective-permute-done | bytes 524320 | tf_op jit(solution)/shard_map/ppermute | solution.py:75
  34.5 4.0 %dynamic-slice_reduce_fusion.1 = (bf16[32,2,1152]{2,1,0:T(2,128)(2,1)S(1)}, bf16[32,2,1152]{2,1,0:T(2,128)(2,1)S(1)}, bf16[32,2,1152]{2,1,0:T(2,128)(2,1)S(1)}, bf16[32,2,1152]{2,1,0:T(2,128)(2,1)S(1)}) fusion(bf16[32,2,4,1152]{3,2,1,0:T(4,128)(2,1)S(1)} %reshape.433, s32[]{:T(128)S(6)} %select_n.300, s32[]{:T(128)S(6)} %select_n.308, s32[]{:T(128)S(6)} %select_n.306, ...), kind=kLoop, calls=%fused_computation.149 | loop fusion | bytes 1179664 | tf_op jit(solution)/shard_map/jit(dynamic_index_in_dim)/dynamic_slice | solution.py:106
  54.8 3.4 collective-permute-done.3
  67.3 4.0 %fusion.43 = f32[1024,768]{1,0:T(8,128)S(1)} fusion(bf16[1024,768]{1,0:T(8,128)(2,1)S(1)} %bitcast.207, bf16[1024,1024]{1,0:T(8,128)(2,1)} %copy-done.8, f32[1024]{0:T(1024)S(1)} %bitcast.243, f32[1024]{0:T(1024)S(1)} %add_rsqrt_fusion), kind=kOutput, calls=%fused_computation.110 | convolution fusion | flops 1614807040 | bytes 6823936 | tf_op jit(solution)/shard_map/dot_general | solution.py:37
  80.3 3.6 %collective-permute-done.12 = bf16[128,1024]{0,1:T(8,128)(2,1)S(1)} collective-permute-done((bf16[128,1024]{0,1:T(8,128)(2,1)S(1)}, bf16[128,1024]{0,1:T(8,128)(2,1)S(1)}, u32[]{:S(2)}, u32[]{:S(2)}) %collective-permute-start.12) | collective-permute-done | bytes 262176 | tf_op jit(solution)/shard_map/ppermute | solution.py:75
  90.8 9.0 %collective-permute-done.15 = bf16[256,1024]{1,0:T(8,128)(2,1)S(1)} collective-permute-done((bf16[256,1024]{1,0:T(8,128)(2,1)S(1)}, bf16[256,1024]{1,0:T(8,128)(2,1)S(1)}, u32[]{:S(2)}, u32[]{:S(2)}) %collective-permute-start.15) | collective-permute-done | bytes 524320 | tf_op jit(solution)/shard_map/ppermute | solution.py:75
  106.7 4.4 %collective-permute-done.17 = bf16[128,1024]{1,0:T(8,128)(2,1)S(1)} collective-permute-done((bf16[128,1024]{1,0:T(8,128)(2,1)S(1)}, bf16[128,1024]{1,0:T(8,128)(2,1)S(1)}, u32[]{:S(2)}, u32[]{:S(2)}) %collective-permute-start.17) | collective-permute-done | bytes 262176 | tf_op jit(solution)/shard_map/ppermute | solution.py:75
  118.2 5.2 %collective-permute-done.19 = bf16[256,1024]{1,0:T(8,128)(2,1)} collective-permute-done((bf16[256,1024]{1,0:T(8,128)(2,1)}, bf16[256,1024]{1,0:T(8,128)(2,1)}, u32[]{:S(2)}, u32[]{:S(2)}) %collective-permute-start.19) | collective-permute-done | bytes 524320 | tf_op jit(solution)/shard_map/ppermute | solution.py:75
  133.3 10.3 %fusion.68 = f32[1024,2304]{1,0:T(8,128)} fusion(bf16[1024,1024]{1,0:T(8,128)(2,1)} %copy-done.47, bf16[1024,2304]{1,0:T(8,128)(2,1)} %bitcast.263), kind=kOutput, calls=%fused_computation.262 | convolution fusion | flops 4831838208 | bytes 16252928 | tf_op jit(solution)/shard_map/dot_general | solution.py:37
  143.6 9.0 %multiply_convert_fusion.2 = (bf16[1024,1152]{1,0:T(8,128)(2,1)S(1)}, bf16[1024,1152]{1,0:T(8,128)(2,1)S(1)}, bf16[1024,1152]{1,0:T(8,128)(2,1)S(1)}) fusion(f32[1024,2304]{1,0:T(8,128)} %fusion.68, bf16[1152,1024]{1,0:T(8,128)(2,1)} %all-gather.6.cloned.1.call-done, bf16[1024,1024]{1,0:T(8,128)(2,1)} %constant_dynamic-update-slice_fusion.7, ...), kind=kOutput, calls=%fused_computation.10 | convolution fusion | flops 2435579904 | bytes 20975616 | tf_op jit(solution)/shard_map/dot_general | solution.py:47
  152.6 5.3 %fusion.14 = bf16[1024,1024]{1,0:T(8,128)(2,1)S(1)} fusion(bf16[1024,2304]{1,0:T(8,128)(2,1)S(1)} %bitcast.264, bf16[1024,1152]{1,0:T(8,128)(2,1)S(1)} %get-tuple-element.170, bf16[1024,1152]{1,0:T(8,128)(2,1)S(1)} %get-tuple-element.169), kind=kOutput, calls=%fused_computation.34 | convolution fusion | flops 4842323968 | bytes 11534336 | tf_op jit(solution)/shard_map/dot_general | solution.py:47
  158.8 4.4 %convolution_convert_fusion.2 = bf16[1152,1024]{1,0:T(8,128)(2,1)S(1)} fusion(bf16[1024,1152]{1,0:T(8,128)(2,1)S(1)} %get-tuple-element.135, bf16[1024,1024]{1,0:T(8,128)(2,1)} %constant_dynamic-update-slice_fusion.7, f32[1024]{0:T(1024)S(1)} %bitcast.261), kind=kOutput, calls=%fused_computation.19 | convolution fusion | flops 2420244480 | bytes 6819840 | tf_op jit(solution)/shard_map/dot_general | solution.py:41
  165.0 5.6 %collective-permute-done.25 = bf16[128,1024]{1,0:T(8,128)(2,1)S(1)} collective-permute-done((bf16[128,1024]{1,0:T(8,128)(2,1)S(1)}, bf16[128,1024]{1,0:T(8,128)(2,1)S(1)}, u32[]{:S(2)}, u32[]{:S(2)}) %collective-permute-start.25) | collective-permute-done | bytes 262176 | tf_op jit(solution)/shard_map/ppermute | solution.py:75
  172.7 3.4 convolution_convert_fusion.1
  205.4 5.6 %collective-permute-done.37 = bf16[128,1024]{1,0:T(8,128)(2,1)S(1)} collective-permute-done((bf16[128,1024]{1,0:T(8,128)(2,1)S(1)}, bf16[128,1024]{1,0:T(8,128)(2,1)S(1)}, u32[]{:S(2)}, u32[]{:S(2)}) %collective-permute-start.37) | collective-permute-done | bytes 262176 | tf_op jit(solution)/shard_map/ppermute | solution.py:75
  236.4 5.2 %convolution_convert_fusion.4 = bf16[1024,768]{1,0:T(8,128)(2,1)} fusion(bf16[1024,256]{1,0:T(8,128)(2,1)} %copy-done.41, bf16[1024,256]{1,0:T(8,128)(2,1)} %copy-done.39, bf16[1024,256]{1,0:T(8,128)(2,1)} %copy-done.40, bf16[1024,1024]{1,0:T(8,128)(2,1)} %copy-done.8, f32[1024]{0:T(1024)S(1)} %bitcast.244, f32[1024]{0:T(1024)S(1)} %copy-done.64), kind=kOutput, calls=%fused_computation.35 | convolution fusion | flops 1620312064 | bytes 5251072 | tf_op jit(solution)/shard_map/dot_general | solution.py:41
  259.4 11.3 %collective-permute-done.45 = bf16[4,1,32,1152]{3,2,0,1:T(8,128)(2,1)S(1)} collective-permute-done((bf16[4,1,32,1152]{3,2,0,1:T(8,128)(2,1)S(1)}, bf16[4,1,32,1152]{3,2,0,1:T(8,128)(2,1)S(1)}, u32[]{:S(2)}, u32[]{:S(2)}) %collective-permute-start.45) | collective-permute-done | bytes 294944 | tf_op jit(solution)/shard_map/ppermute | solution.py:75
  270.8 5.8 %collective-permute-done.46 = bf16[4,2,32,1152]{3,2,0,1:T(8,128)(2,1)S(1)} collective-permute-done((bf16[4,2,32,1152]{3,2,0,1:T(8,128)(2,1)S(1)}, bf16[4,2,32,1152]{3,2,0,1:T(8,128)(2,1)S(1)}, u32[]{:S(2)}, u32[]{:S(2)}) %collective-permute-start.46) | collective-permute-done | bytes 589856 | tf_op jit(solution)/shard_map/ppermute | solution.py:75
  281.2 10.8 %collective-permute-done.48 = bf16[4,1,32,1152]{3,2,0,1:T(8,128)(2,1)S(1)} collective-permute-done((bf16[4,1,32,1152]{3,2,0,1:T(8,128)(2,1)S(1)}, bf16[4,1,32,1152]{3,2,0,1:T(8,128)(2,1)S(1)}, u32[]{:S(2)}, u32[]{:S(2)}) %collective-permute-start.48) | collective-permute-done | bytes 294944 | tf_op jit(solution)/shard_map/ppermute | solution.py:75
  292.1 6.8 %collective-permute-done.47 = bf16[4,2,32,1152]{3,2,1,0:T(8,128)(2,1)S(1)} collective-permute-done((bf16[4,2,32,1152]{3,2,1,0:T(8,128)(2,1)S(1)}, bf16[4,2,32,1152]{3,2,1,0:T(8,128)(2,1)S(1)}, u32[]{:S(2)}, u32[]{:S(2)}) %collective-permute-start.47) | collective-permute-done | bytes 589856 | tf_op jit(solution)/shard_map/ppermute | solution.py:75
  302.8 9.7 %collective-permute-done.55 = bf16[4,1,32,1152]{3,2,1,0:T(8,128)(2,1)S(1)} collective-permute-done((bf16[4,1,32,1152]{3,2,1,0:T(8,128)(2,1)S(1)}, bf16[4,1,32,1152]{3,2,1,0:T(8,128)(2,1)S(1)}, u32[]{:S(2)}, u32[]{:S(2)}) %collective-permute-start.55) | collective-permute-done | bytes 294944 | tf_op jit(solution)/shard_map/ppermute | solution.py:75
  316.7 5.1 %collective-permute-done.56 = bf16[32,3200]{1,0:T(8,128)(2,1)S(1)} collective-permute-done((bf16[32,3200]{1,0:T(8,128)(2,1)S(1)}, bf16[32,3200]{1,0:T(8,128)(2,1)S(1)}, u32[]{:S(2)}, u32[]{:S(2)}) %collective-permute-start.56) | collective-permute-done | bytes 204832 | tf_op jit(solution)/shard_map/ppermute | solution.py:75
  321.8 3.2 collective-permute-done.57
  339.1 3.9 %multiply_subtract_fusion = (f32[573600]{0:T(1024)}, f32[573600]{0:T(1024)}) fusion(f32[573600]{0:T(1024)S(1)} %copy-done.3, f32[573600]{0:T(1024)S(1)} %constant_dynamic-update-slice_fusion.17, f32[573600]{0:T(1024)S(1)} %copy-done.22, f32[573600]{0:T(1024)S(1)} %copy-done.23), kind=kLoop, calls=%fused_computation.31 | loop fusion | flops 9751200 | bytes 13766400 | tf_op jit(solution)/shard_map/sub | solution.py:325
  (450 shorter events, 187.0 us)
Async XLA Ops:
  7.2 54.0 %all-gather.4.cloned.1.call-start = ((), (), s32[]{:S(2)}) async-start(), calls=%async_computation | async-start | bytes 2654208 | tf_op jit(solution)/shard_map/all_gather | solution.py:115
  20.2 113.1 %all-gather.8.cloned.1.call-start = ((), (), s32[]{:S(2)}) async-start(), calls=%async_computation.2 | async-start | bytes 5308416 | tf_op jit(solution)/shard_map/all_gather | solution.py:115
  47.4 96.3 %all-gather.6.cloned.1.call-start = ((), (), s32[]{:S(2)}) async-start(), calls=%async_computation.1 | async-start | bytes 2654208 | tf_op jit(solution)/shard_map/all_gather | solution.py:115
  62.6 15.9 %collective-permute-start.8 = (bf16[256,1024]{0,1:T(8,128)(2,1)S(1)}, bf16[256,1024]{0,1:T(8,128)(2,1)S(1)}, u32[]{:S(2)}, u32[]{:S(2)}) collective-permute-start(bf16[256,1024]{0,1:T(8,128)(2,1)S(1)} %bitcast.189), channel_id=1, source_target_pairs={{0,8},{1,9},{2,10},{3,11},{4,12},{5,13},{6,14},{7,15},{8,0},{9,1},... | collective-permute-start | bytes 1572872 | tf_op jit(solution)/shard_map/ppermute | solution.py:75
  63.6 13.8 %collective-permute-start.10 = (bf16[256,1024]{0,1:T(8,128)(2,1)S(1)}, bf16[256,1024]{0,1:T(8,128)(2,1)S(1)}, u32[]{:S(2)}, u32[]{:S(2)}) collective-permute-start(bf16[256,1024]{0,1:T(8,128)(2,1)S(1)} %bitcast.190), channel_id=1, source_target_pairs={{0,16},{1,17},{2,18},{3,19},{4,20},{5,21},{6,22},{7,23},{8,24},{9,... | collective-permute-start | bytes 1572872 | tf_op jit(solution)/shard_map/ppermute | solution.py:75
  176.3 26.5 %collective-permute-start.34 = (bf16[4,4,32,1152]{3,2,1,0:T(8,128)(2,1)S(1)}, bf16[4,4,32,1152]{3,2,1,0:T(8,128)(2,1)S(1)}, u32[]{:S(2)}, u32[]{:S(2)}) collective-permute-start(bf16[4,4,32,1152]{3,2,1,0:T(8,128)(2,1)S(1)} %dynamic-slice_bitcast_fusion.2), channel_id=1, source_target_pairs={{0,4},{1,5},{2,6},{3,7},{4,0},{5,1},{6,2},{7,3},{8,12},{9,13},{10,... | collective-permute-start | bytes 3538952 | tf_op jit(solution)/shard_map/ppermute | solution.py:75
  187.8 33.9 %collective-permute-start.33 = (bf16[2,144,1024]{2,1,0:T(8,128)(2,1)S(1)}, bf16[2,144,1024]{2,1,0:T(8,128)(2,1)S(1)}, u32[]{:S(2)}, u32[]{:S(2)}) collective-permute-start(bf16[2,144,1024]{2,1,0:T(8,128)(2,1)S(1)} %dynamic-slice_bitcast_fusion.5), channel_id=1, source_target_pairs={{0,1},{1,0},{2,3},{3,2},{4,5},{5,4},{6,7},{7,6},{8,9},{9,8},{10,11... | collective-permute-start | bytes 1769480 | tf_op jit(solution)/shard_map/ppermute | solution.py:75
  189.4 33.4 %collective-permute-start.31 = (bf16[256,256]{1,0:T(8,128)(2,1)S(1)}, bf16[256,256]{1,0:T(8,128)(2,1)S(1)}, u32[]{:S(2)}, u32[]{:S(2)}) collective-permute-start(bf16[256,256]{1,0:T(8,128)(2,1)S(1)} %convolution_convert_fusion.10), channel_id=1, source_target_pairs={{0,16},{1,17},{2,18},{3,19},{4,20},{5,21},{6,22},{7,23},{8,24},{9,... | collective-permute-start | bytes 393224 | tf_op jit(solution)/shard_map/ppermute | solution.py:75
  191.0 31.8 %collective-permute-start.32 = (bf16[256,256]{1,0:T(8,128)(2,1)S(1)}, bf16[256,256]{1,0:T(8,128)(2,1)S(1)}, u32[]{:S(2)}, u32[]{:S(2)}) collective-permute-start(bf16[256,256]{1,0:T(8,128)(2,1)S(1)} %convolution_convert_fusion.9), channel_id=1, source_target_pairs={{0,24},{1,25},{2,26},{3,27},{4,28},{5,29},{6,30},{7,31},{8,16},{9,... | collective-permute-start | bytes 393224 | tf_op jit(solution)/shard_map/ppermute | solution.py:75
  214.5 38.9 %collective-permute-start.44 = (bf16[4,4,32,1152]{3,2,1,0:T(8,128)(2,1)}, bf16[4,4,32,1152]{3,2,1,0:T(8,128)(2,1)}, u32[]{:S(2)}, u32[]{:S(2)}) collective-permute-start(bf16[4,4,32,1152]{3,2,1,0:T(8,128)(2,1)} %dynamic-slice_bitcast_fusion), channel_id=1, source_target_pairs={{0,4},{1,5},{2,6},{3,7},{4,0},{5,1},{6,2},{7,3},{8,12},{9,13},{10,... | collective-permute-start | bytes 3538952 | tf_op jit(solution)/shard_map/ppermute | solution.py:75
  217.5 24.1 %collective-permute-start.36 = (bf16[256,1024]{1,0:T(8,128)(2,1)}, bf16[256,1024]{1,0:T(8,128)(2,1)}, u32[]{:S(2)}, u32[]{:S(2)}) collective-permute-start(bf16[256,1024]{1,0:T(8,128)(2,1)} %pad_maximum_fusion.10), channel_id=1, source_target_pairs={{0,8},{1,9},{2,10},{3,11},{4,12},{5,13},{6,14},{7,15},{8,0},{9,1},... | collective-permute-start | bytes 1572872 | tf_op jit(solution)/shard_map/ppermute | solution.py:75
  221.7 21.1 %collective-permute-start.38 = (bf16[256,1024]{1,0:T(8,128)(2,1)}, bf16[256,1024]{1,0:T(8,128)(2,1)}, u32[]{:S(2)}, u32[]{:S(2)}) collective-permute-start(bf16[256,1024]{1,0:T(8,128)(2,1)} %pad_maximum_fusion.11), channel_id=1, source_target_pairs={{0,16},{1,17},{2,18},{3,19},{4,20},{5,21},{6,22},{7,23},{8,24},{9,... | collective-permute-start | bytes 1572872 | tf_op jit(solution)/shard_map/ppermute | solution.py:75
  231.7 20.5 %collective-permute-start.43 = (bf16[4,2,32,1152]{3,2,0,1:T(8,128)(2,1)}, bf16[4,2,32,1152]{3,2,0,1:T(8,128)(2,1)}, u32[]{:S(2)}, u32[]{:S(2)}) collective-permute-start(bf16[4,2,32,1152]{3,2,0,1:T(8,128)(2,1)} %bitcast.186), channel_id=1, source_target_pairs={{0,1},{1,0},{2,3},{3,2},{4,5},{5,4},{6,7},{7,6},{8,9},{9,8},{10,11... | collective-permute-start | bytes 1769480 | tf_op jit(solution)/shard_map/ppermute | solution.py:75
  232.5 18.5 %collective-permute-start.42 = (bf16[1,144,1024]{2,1,0:T(8,128)(2,1)}, bf16[1,144,1024]{2,1,0:T(8,128)(2,1)}, u32[]{:S(2)}, u32[]{:S(2)}) collective-permute-start(bf16[1,144,1024]{2,1,0:T(8,128)(2,1)} %constant_dynamic-slice_fusion.7), channel_id=1, source_target_pairs={{0,2},{1,3},{2,0},{3,1},{4,6},{5,7},{6,4},{7,5},{8,10},{9,11},{10,... | collective-permute-start | bytes 884744 | tf_op jit(solution)/shard_map/ppermute | solution.py:75
  248.3 28.5 %collective-permute-start.39 = (bf16[4,4,32,1152]{3,2,1,0:T(8,128)(2,1)S(1)}, bf16[4,4,32,1152]{3,2,1,0:T(8,128)(2,1)S(1)}, u32[]{:S(2)}, u32[]{:S(2)}) collective-permute-start(bf16[4,4,32,1152]{3,2,1,0:T(8,128)(2,1)S(1)} %dynamic-slice_bitcast_fusion.1), channel_id=1, source_target_pairs={{0,4},{1,5},{2,6},{3,7},{4,0},{5,1},{6,2},{7,3},{8,12},{9,13},{10,... | collective-permute-start | bytes 3538952 | tf_op jit(solution)/shard_map/ppermute | solution.py:75
  255.0 15.7 %collective-permute-start.45 = (bf16[4,1,32,1152]{3,2,0,1:T(8,128)(2,1)S(1)}, bf16[4,1,32,1152]{3,2,0,1:T(8,128)(2,1)S(1)}, u32[]{:S(2)}, u32[]{:S(2)}) collective-permute-start(bf16[4,1,32,1152]{3,2,0,1:T(8,128)(2,1)S(1)} %constant_dynamic-slice_fusion.4), channel_id=1, source_target_pairs={{0,2},{1,3},{2,0},{3,1},{4,6},{5,7},{6,4},{7,5},{8,10},{9,11},{10,... | collective-permute-start | bytes 884744 | tf_op jit(solution)/shard_map/ppermute | solution.py:75
  255.7 20.9 %collective-permute-start.46 = (bf16[4,2,32,1152]{3,2,0,1:T(8,128)(2,1)S(1)}, bf16[4,2,32,1152]{3,2,0,1:T(8,128)(2,1)S(1)}, u32[]{:S(2)}, u32[]{:S(2)}) collective-permute-start(bf16[4,2,32,1152]{3,2,0,1:T(8,128)(2,1)S(1)} %bitcast.215), channel_id=1, source_target_pairs={{0,1},{1,0},{2,3},{3,2},{4,5},{5,4},{6,7},{7,6},{8,9},{9,8},{10,11... | collective-permute-start | bytes 1769480 | tf_op jit(solution)/shard_map/ppermute | solution.py:75
  258.5 40.6 %collective-permute-start.49 = (bf16[256,1024]{1,0:T(8,128)(2,1)S(1)}, bf16[256,1024]{1,0:T(8,128)(2,1)S(1)}, u32[]{:S(2)}, u32[]{:S(2)}) collective-permute-start(bf16[256,1024]{1,0:T(8,128)(2,1)S(1)} %pad_maximum_fusion.12), channel_id=1, source_target_pairs={{0,8},{1,9},{2,10},{3,11},{4,12},{5,13},{6,14},{7,15},{8,0},{9,1},... | collective-permute-start | bytes 1572872 | tf_op jit(solution)/shard_map/ppermute | solution.py:75
  258.5 40.6 %collective-permute-start.50 = (bf16[256,1024]{1,0:T(8,128)(2,1)S(1)}, bf16[256,1024]{1,0:T(8,128)(2,1)S(1)}, u32[]{:S(2)}, u32[]{:S(2)}) collective-permute-start(bf16[256,1024]{1,0:T(8,128)(2,1)S(1)} %pad_maximum_fusion.13), channel_id=1, source_target_pairs={{0,16},{1,17},{2,18},{3,19},{4,20},{5,21},{6,22},{7,23},{8,24},{9,... | collective-permute-start | bytes 1572872 | tf_op jit(solution)/shard_map/ppermute | solution.py:75
  277.1 15.0 %collective-permute-start.48 = (bf16[4,1,32,1152]{3,2,0,1:T(8,128)(2,1)S(1)}, bf16[4,1,32,1152]{3,2,0,1:T(8,128)(2,1)S(1)}, u32[]{:S(2)}, u32[]{:S(2)}) collective-permute-start(bf16[4,1,32,1152]{3,2,0,1:T(8,128)(2,1)S(1)} %constant_dynamic-slice_fusion.1), channel_id=1, source_target_pairs={{0,2},{1,3},{2,0},{3,1},{4,6},{5,7},{6,4},{7,5},{8,10},{9,11},{10,... | collective-permute-start | bytes 884744 | tf_op jit(solution)/shard_map/ppermute | solution.py:75
  279.2 19.7 %collective-permute-start.47 = (bf16[4,2,32,1152]{3,2,1,0:T(8,128)(2,1)S(1)}, bf16[4,2,32,1152]{3,2,1,0:T(8,128)(2,1)S(1)}, u32[]{:S(2)}, u32[]{:S(2)}) collective-permute-start(bf16[4,2,32,1152]{3,2,1,0:T(8,128)(2,1)S(1)} %dynamic-slice_bitcast_fusion.4), channel_id=1, source_target_pairs={{0,1},{1,0},{2,3},{3,2},{4,5},{5,4},{6,7},{7,6},{8,9},{9,8},{10,11... | collective-permute-start | bytes 1769480 | tf_op jit(solution)/shard_map/ppermute | solution.py:75
  299.2 13.4 %collective-permute-start.55 = (bf16[4,1,32,1152]{3,2,1,0:T(8,128)(2,1)S(1)}, bf16[4,1,32,1152]{3,2,1,0:T(8,128)(2,1)S(1)}, u32[]{:S(2)}, u32[]{:S(2)}) collective-permute-start(bf16[4,1,32,1152]{3,2,1,0:T(8,128)(2,1)S(1)} %constant_dynamic-slice_fusion), channel_id=1, source_target_pairs={{0,2},{1,3},{2,0},{3,1},{4,6},{5,7},{6,4},{7,5},{8,10},{9,11},{10,... | collective-permute-start | bytes 884744 | tf_op jit(solution)/shard_map/ppermute | solution.py:75
  299.7 43.3 %collective-permute-start.53 = (bf16[256,1024]{1,0:T(8,128)(2,1)}, bf16[256,1024]{1,0:T(8,128)(2,1)}, u32[]{:S(2)}, u32[]{:S(2)}) collective-permute-start(bf16[256,1024]{1,0:T(8,128)(2,1)} %pad_maximum_fusion.14), channel_id=1, source_target_pairs={{0,8},{1,9},{2,10},{3,11},{4,12},{5,13},{6,14},{7,15},{8,0},{9,1},... | collective-permute-start | bytes 1572872 | tf_op jit(solution)/shard_map/ppermute | solution.py:75
  300.8 42.2 %collective-permute-start.54 = (bf16[256,1024]{1,0:T(8,128)(2,1)}, bf16[256,1024]{1,0:T(8,128)(2,1)}, u32[]{:S(2)}, u32[]{:S(2)}) collective-permute-start(bf16[256,1024]{1,0:T(8,128)(2,1)} %pad_maximum_fusion.15), channel_id=1, source_target_pairs={{0,16},{1,17},{2,18},{3,19},{4,20},{5,21},{6,22},{7,23},{8,24},{9,... | collective-permute-start | bytes 1572872 | tf_op jit(solution)/shard_map/ppermute | solution.py:75
  (110 other events, 694.0 us)
Sparse Core Ops, SparseCore 0:
  20.4 31.9 all-gather.3
  53.9 50.7 all-gather.7
  106.3 30.4 all-gather.5
